TPU v7x, 32 devices: a whole 2x2x4 slice. The times are simulated.
32 devices in a mesh: group: 2 (over x), dom: 16 (over z, y, core).
Axes of the slice: x: 2, y: 2, z: 4, core: 2. Of those that a mesh axis runs over, the one named last changes fastest.
Arguments:
- matrices: bfloat16 [4, 768, 6, 128, 128], P(None, ('group', 'dom')), parts along dimension 1, may hold values from -0.21875 to 0.21875
- values: bfloat16 [98304, 256], P(('group', 'dom')), parts along dimension 0, may hold values from -6 to 6
- exponents: int32 [768], P(('group', 'dom')), parts along dimension 0, may hold values from -2 to 2
- pattern: int32 [4, 768, 6], P(None, ('group', 'dom')), parts along dimension 1, may hold values from 0 to 87, as said below
- block_counts: int32 [4, 768], P(None, ('group', 'dom')), parts along dimension 1, may hold values from 1 to 6
- send_lists: int32 [32, 16, 4], P(('group', 'dom')), parts along dimension 0, may hold values from 0 to 23, as said below
- ghost_counts: int32 [32, 16], P(('group', 'dom')), parts along dimension 0, may hold values from 0 to 4, as said below
Outputs:
- reduced: float32 [2048, 256], P(('group', 'dom')), parts along dimension 0
There are 2 independent parts, one for each index of `group`. A program takes and returns all parts, laid end to end along the dimension named above; each array names one. Nothing has to cross between parts.
Inputs may be any that keep to these rules, and one draw needn't show every extreme that they name: `pattern`: every entry names a slot below 24 (an own block) or 24 + p * 4 + g with g below ghost_counts[p, d] for the partition d that holds the row; slot k = 0 is the row block's own diagonal block. `send_lists`: the 4 entries of one pair are distinct. `ghost_counts`: zero for a partition and itself; at most 1 for partitions p, r with |p - r| other than 1; at least 1 for adjacent partitions.
All inputs are finite; a program needn't handle non-finite values.
Results may differ from a plain program's by a relative error of at most 0.0029.
Values may be sent and summed in bfloat16 or wider, within the bound.
No kernel may reach another device: no remote copies, remote signals or barrier semaphores. Data moves between devices by JAX's collectives and lax.ppermute only.
A program may use at most 192 MiB of HBM per device.

v0:
```python
import math

import jax
import jax.numpy as jnp
from jax import lax
from jax.sharding import PartitionSpec as P


def pick_blocks(source, listing, counts):
    chosen = source[listing.reshape(-1)].reshape(listing.shape + source.shape[1:])
    listed = jnp.arange(listing.shape[1])[None, :] < counts[:, None]
    return jnp.where(listed[:, :, None, None], chosen, jnp.zeros((), source.dtype))


def on_device(matrices, values, exponents, pattern, block_counts, send_lists, ghost_counts):
    row_count, columns = values.shape
    block_size = matrices.shape[-1]
    owned_count = exponents.shape[0]
    factor = jnp.exp2(exponents.astype(jnp.float32)).astype(jnp.bfloat16)
    owned_blocks = values.reshape(owned_count, block_size, columns) * factor[:, None, None]
    partitions = lax.axis_size("dom")
    listing = send_lists[0]
    counts = ghost_counts[0]
    outgoing = pick_blocks(owned_blocks, listing, counts)
    incoming = lax.all_to_all(outgoing, "dom", split_axis=0, concat_axis=0, tiled=True)
    lookup = jnp.concatenate([owned_blocks, incoming.reshape(-1, block_size, columns)], 0)
    slot_steps = jnp.arange(pattern.shape[2])
    flat_owned = owned_blocks.reshape(-1, columns)
    partials = []
    for which in range(pattern.shape[0]):
        gathered = lookup[pattern[which].reshape(-1)].reshape(
            owned_count, pattern.shape[2], block_size, columns
        )
        present = slot_steps[None, :] < block_counts[which][:, None]
        gathered = jnp.where(present[:, :, None, None], gathered, jnp.zeros((), jnp.bfloat16))
        product = jnp.einsum(
            "bkij,bkjr->bir", matrices[which], gathered, preferred_element_type=jnp.float32
        ).astype(jnp.bfloat16)
        partials.append(
            lax.dot_general(
                flat_owned,
                product.reshape(-1, columns),
                (((0,), (0,)), ((), ())),
                preferred_element_type=jnp.float32,
            )
        )
    stacked = jnp.stack(partials).reshape(-1, columns)
    summed = lax.psum_scatter(stacked, "dom", scatter_dimension=0, tiled=True)
    return summed * (1.0 / math.sqrt(row_count * partitions))


def solution(mesh):
    return jax.shard_map(
        on_device,
        mesh=mesh,
        in_specs=(
            P(None, ("group", "dom"), None, None, None),
            P(("group", "dom"), None),
            P(("group", "dom")),
            P(None, ("group", "dom"), None),
            P(None, ("group", "dom")),
            P(("group", "dom"), None, None),
            P(("group", "dom"), None),
        ),
        out_specs=P(("group", "dom"), None),
        check_vma=False,
    )
```

profile of v0, /device:TPU:0, one launch (start us, length us, event | category | flops | bytes accessed | tf_op | source)
XLA Modules:
  0.0 259.4 jit_solution(11621079898713298110)
XLA Ops:
  6.5 1.9 copy.10
  8.5 0.7 exponential_convert_fusion
  9.1 0.8 copy.11
  9.9 0.1 reshape_squeeze.15
  10.0 0.7 iota_compare_fusion.4
  10.7 0.2 broadcast_multiply_fusion
  10.9 3.0 %gather_fusion = bf16[64,128,256]{1,2,0:T(8,128)(2,1)} fusion(bf16[24,128,256]{1,2,0:T(8,128)(2,1)S(1)} %broadcast_multiply_fusion, s32[1024]{0:T(1024)S(1)} %pad_clamp_fusion.4), kind=kCustom, calls=%fused_computation | custom fusion | bytes 8388864 | tf_op jit(solution)/shard_map/gather | solution.py:10
  13.9 4.5 %broadcast_select_fusion = bf16[16,4,128,256]{2,3,1,0:T(8,128)(2,1)} fusion(bf16[16,4,128,256]{2,3,1,0:T(8,128)(2,1)} %bitcast.139, pred[16,4]{1,0:T(8,128)(4,1)S(1)} %iota_compare_fusion.4), kind=kLoop, calls=%fused_computation.30 | loop fusion | flops 2097152 | bytes 8388672 | tf_op jit(solution)/shard_map/jit(_where)/select_n | solution.py:12
  18.4 0.0 copy-start
  18.4 0.0 copy-start.1
  18.4 7.6 %all-to-all-start = ((bf16[16,4,128,256]{2,3,1,0:T(8,128)(2,1)}), bf16[16,4,128,256]{2,3,1,0:T(8,128)(2,1)}, u32[]{:S(2)}, u32[]{:S(2)}) async-start(bf16[16,4,128,256]{2,3,1,0:T(8,128)(2,1)} %broadcast_select_fusion), calls=%async_computation | async-start | bytes 8388608 | tf_op jit(solution)/shard_map/all_to_all | solution.py:25
  26.0 0.0 reduce-scatter.2.cloned.1.call-start
  26.1 0.0 copy-done
  26.1 0.1 copy.12
  26.2 0.1 reshape_squeeze.16
  26.3 0.1 copy.13
  26.4 0.1 reshape_squeeze.17
  26.5 0.1 copy.14
  26.6 0.1 reshape_squeeze.18
  26.7 0.1 copy.15
  26.7 0.1 reshape_squeeze.19
  26.9 0.0 copy-done.1
  27.0 0.1 iota_compare_fusion.2
  27.0 0.1 iota_compare_fusion
  27.1 76.6 %all-to-all-done = bf16[16,4,128,256]{2,3,1,0:T(8,128)(2,1)} async-done(((bf16[16,4,128,256]{2,3,1,0:T(8,128)(2,1)}), bf16[16,4,128,256]{2,3,1,0:T(8,128)(2,1)}, u32[]{:S(2)}, u32[]{:S(2)}) %all-to-all-start) | async-done | bytes 4194336 | tf_op jit(solution)/shard_map/all_to_all | solution.py:25
  103.7 5.1 %pad_maximum_fusion = bf16[88,128,256]{1,2,0:T(8,128)(2,1)} fusion(bf16[64,128,256]{1,2,0:T(8,128)(2,1)} %bitcast.5, bf16[24,128,256]{1,2,0:T(8,128)(2,1)S(1)} %broadcast_multiply_fusion), kind=kLoop, calls=%fused_computation.17 | loop fusion | flops 2883584 | bytes 11534336 | tf_op jit(solution)/shard_map/concatenate | solution.py:26
  108.8 10.0 %gather_fusion.1 = bf16[144,128,256]{1,2,0:T(8,128)(2,1)} fusion(bf16[88,128,256]{1,2,0:T(8,128)(2,1)} %pad_maximum_fusion, s32[1024]{0:T(1024)S(1)} %pad_clamp_fusion.3), kind=kCustom, calls=%fused_computation.1 | custom fusion | bytes 18874944 | tf_op jit(solution)/shard_map/gather | solution.py:31
  118.8 10.0 %gather_fusion.2 = bf16[144,128,256]{1,2,0:T(8,128)(2,1)} fusion(bf16[88,128,256]{1,2,0:T(8,128)(2,1)} %pad_maximum_fusion, s32[1024]{0:T(1024)S(1)} %pad_clamp_fusion.2), kind=kCustom, calls=%fused_computation.2 | custom fusion | bytes 18874944 | tf_op jit(solution)/shard_map/gather | solution.py:31
  128.8 9.9 %gather_fusion.3 = bf16[144,128,256]{1,2,0:T(8,128)(2,1)} fusion(bf16[88,128,256]{1,2,0:T(8,128)(2,1)} %pad_maximum_fusion, s32[1024]{0:T(1024)S(1)} %pad_clamp_fusion.1), kind=kCustom, calls=%fused_computation.3 | custom fusion | bytes 18874944 | tf_op jit(solution)/shard_map/gather | solution.py:31
  138.6 9.9 %gather_fusion.4 = bf16[144,128,256]{1,2,0:T(8,128)(2,1)} fusion(bf16[88,128,256]{1,2,0:T(8,128)(2,1)} %pad_maximum_fusion, s32[1024]{0:T(1024)S(1)} %pad_clamp_fusion), kind=kCustom, calls=%fused_computation.4 | custom fusion | bytes 18874944 | tf_op jit(solution)/shard_map/gather | solution.py:31
  148.5 7.2 %fusion.80 = f32[1,256,256]{2,1,0:T(8,128)S(1)} fusion(bf16[24,128,256]{1,2,0:T(8,128)(2,1)S(1)} %broadcast_multiply_fusion, bf16[4,24,6,128,128]{4,3,2,1,0:T(8,128)(2,1)} %param.7, bf16[24,6,128,256]{2,3,1,0:T(8,128)(2,1)} %bitcast.143, pred[24,6]{1,0:T(8,128)(4,1)S(1)} %get-tuple-element.16), kind=kOutput, calls=%fused_computation.43 | convolution fusion | flops 1616117760 | bytes 15990928 | tf_op jit(solution)/shard_map/dot_general | solution.py:40
  155.8 7.2 %fusion.87 = f32[1,256,256]{2,1,0:T(8,128)S(1)} fusion(bf16[24,128,256]{1,2,0:T(8,128)(2,1)S(1)} %broadcast_multiply_fusion, bf16[4,24,6,128,128]{4,3,2,1,0:T(8,128)(2,1)} %param.7, bf16[24,6,128,256]{2,3,1,0:T(8,128)(2,1)} %bitcast.142, pred[24,6]{1,0:T(8,128)(4,1)S(1)} %get-tuple-element.15), kind=kOutput, calls=%fused_computation.44 | convolution fusion | flops 1616117760 | bytes 15990928 | tf_op jit(solution)/shard_map/dot_general | solution.py:40
  163.0 7.2 %fusion.94 = f32[1,256,256]{2,1,0:T(8,128)S(1)} fusion(bf16[24,128,256]{1,2,0:T(8,128)(2,1)S(1)} %broadcast_multiply_fusion, bf16[4,24,6,128,128]{4,3,2,1,0:T(8,128)(2,1)} %param.7, bf16[24,6,128,256]{2,3,1,0:T(8,128)(2,1)} %bitcast.141, pred[24,6]{1,0:T(8,128)(4,1)S(1)} %get-tuple-element.14), kind=kOutput, calls=%fused_computation.45 | convolution fusion | flops 1616117760 | bytes 15990928 | tf_op jit(solution)/shard_map/dot_general | solution.py:40
  170.3 7.2 %fusion.101 = f32[1,256,256]{2,1,0:T(8,128)S(1)} fusion(bf16[24,128,256]{1,2,0:T(8,128)(2,1)S(1)} %broadcast_multiply_fusion, bf16[4,24,6,128,128]{4,3,2,1,0:T(8,128)(2,1)} %param.7, bf16[24,6,128,256]{2,3,1,0:T(8,128)(2,1)} %bitcast.140, pred[24,6]{1,0:T(8,128)(4,1)S(1)} %get-tuple-element.13), kind=kOutput, calls=%fused_computation.46 | convolution fusion | flops 1616117760 | bytes 15990928 | tf_op jit(solution)/shard_map/dot_general | solution.py:40
  177.5 1.0 pad_maximum_fusion.1
  178.6 0.0 reduce-scatter.2.cloned.1.call-update
  178.6 72.5 %reduce-scatter.2.cloned.1.call-done = f32[64,256]{1,0:T(8,128)} async-done(((f32[1024,256]{1,0:T(8,128)}), f32[64,256]{1,0:T(8,128)}) %reduce-scatter.2.cloned.1.call-update) | async-done | bytes 65552 | tf_op jit(solution)/shard_map/reduce_scatter | solution.py:48
  251.1 1.5 broadcast_multiply_fusion.1
  (12 shorter events, 0.1 us)
Async XLA Ops:
  18.4 7.6 %copy-start = (s32[4,24,6]{1,0,2:T(4,128)S(1)}, s32[4,24,6]{1,0,2:T(4,128)}, u32[]{:S(2)}) copy-start(s32[4,24,6]{1,0,2:T(4,128)} %param.10) | copy-start | bytes 6916
  18.4 8.5 %copy-start.1 = (s32[4,24]{1,0:T(4,128)S(1)}, s32[4,24]{1,0:T(4,128)}, u32[]{:S(2)}) copy-start(s32[4,24]{1,0:T(4,128)} %param.11) | copy-start | bytes 1156
  18.4 85.3 %all-to-all-start = ((bf16[16,4,128,256]{2,3,1,0:T(8,128)(2,1)}), bf16[16,4,128,256]{2,3,1,0:T(8,128)(2,1)}, u32[]{:S(2)}, u32[]{:S(2)}) async-start(bf16[16,4,128,256]{2,3,1,0:T(8,128)(2,1)} %broadcast_select_fusion), calls=%async_computation | async-start | bytes 8388608 | tf_op jit(solution)/shard_map/all_to_all | solution.py:25
  26.0 225.1 %reduce-scatter.2.cloned.1.call-start = ((), (), s32[]{:S(2)}) async-start(), calls=%async_computation.2 | async-start | bytes 1114112 | tf_op jit(solution)/shard_map/reduce_scatter | solution.py:48
Sparse Core Ops, SparseCore 0:
  178.7 72.3 reduce-scatter.1
where the time goes:
time: 260 us; the launch traced here: 259 us
  waiting for transfers between devices  149 us (57%)
  local copies, waits for them, and re-layouts  46.2 us (18%)
  matrix products  29 us (11%)
  other arithmetic  13.9 us (5%)
  between operations  13.6 us (5%)
  starting transfers between devices  7.61 us (3%)
    all_to_all x1, waiting for transfers between devices, on_device(): lax.all_to_all(outgoing, 'dom', split_axis=0, concat_axis=0, tiled=True)  76.6 us
    reduce_scatter x1, waiting for transfers between devices, on_device(): summed = lax.psum_scatter(stacked, 'dom', scatter_dimension=0, tiled=True)  72.5 us
    gather x4, local copies, waits for them, and re-layouts, on_device(): lookup[pattern[which].reshape(-1)]  39.7 us
    dot_general x4, matrix products, on_device(): lax.dot_general(flat_owned, product.reshape(-1, columns), (((0,), (0,)),...  29 us
    all_to_all x1, starting transfers between devices, on_device(): lax.all_to_all(outgoing, 'dom', split_axis=0, concat_axis=0, tiled=True)  7.57 us
  transfers between devices with their start and end apart: 2, of which 2 were waited for; matrix products, arithmetic and copies ran while one was open for 0% of the time, Pallas kernels for 0%

commit v1 on v0

v1 whole, which is shorter than its diff:
```python
import functools
import math

import jax
import jax.numpy as jnp
from jax import lax
from jax.experimental import pallas as pl
from jax.experimental.pallas import tpu as pltpu
from jax.sharding import PartitionSpec as P

SMEM = pl.BlockSpec(memory_space=pltpu.SMEM)
HBM = pl.BlockSpec(memory_space=pl.ANY)


def power_of_two(exponent):
    return lax.shift_left(jnp.int32(1), exponent + 2).astype(jnp.float32) * 0.25


def pack_kernel(parts, size, lists, exponents, values, far, after, before, held, came, went):
    me = lax.axis_index("dom")
    lent = lists.shape[2]
    upper = jnp.minimum(me + 1, parts - 1)
    lower = jnp.maximum(me - 1, 0)
    places = [(lists[0, p, 0], far.at[p]) for p in range(parts)]
    places += [(lists[0, upper, g], after.at[g - 1]) for g in range(1, lent)]
    places += [(lists[0, lower, g], before.at[g - 1]) for g in range(1, lent)]
    incoming, outgoing = [], []
    for n, (block, place) in enumerate(places):
        rows = pl.ds(pl.multiple_of(block * size, size), size)
        incoming.append(pltpu.make_async_copy(values.at[rows, :], held.at[n], came.at[n]))
        incoming[-1].start()
    for n, (block, place) in enumerate(places):
        incoming[n].wait()
        factor = power_of_two(exponents[block]).astype(jnp.bfloat16)
        held[n] = held[n] * factor
        outgoing.append(pltpu.make_async_copy(held.at[n], place, went.at[n]))
        outgoing[-1].start()
    for copy in outgoing:
        copy.wait()


def pack(lists, exponents, values, size):
    parts, lent = lists.shape[1:]
    columns = values.shape[1]
    blocks = parts + 2 * (lent - 1)
    block = lambda n: jax.ShapeDtypeStruct((n, size, columns), values.dtype)
    return pl.pallas_call(
        functools.partial(pack_kernel, parts, size),
        out_shape=(block(parts), block(lent - 1), block(lent - 1)),
        in_specs=[SMEM, SMEM, HBM],
        out_specs=(HBM, HBM, HBM),
        scratch_shapes=[
            pltpu.VMEM((blocks, size, columns), values.dtype),
            pltpu.SemaphoreType.DMA((blocks,)),
            pltpu.SemaphoreType.DMA((blocks,)),
        ],
        name="pack",
    )(lists, exponents, values)


def project_kernel(ghosts, slots, counts, exponents, values, matrices, weights, partial, acc, basis, staged, went):
    step = pl.program_id(0)
    terms, owned, kept = slots.shape
    size, columns = values.shape

    @pl.when(step == 0)
    def _():
        def clear(n, carry):
            acc[n] = jnp.zeros(acc.shape[1:], acc.dtype)
            return carry
        lax.fori_loop(0, acc.shape[0], clear, 0)

    scaled = values[...] * power_of_two(exponents[step]).astype(jnp.bfloat16)
    basis[pl.ds(pl.multiple_of(step * size, size), size), :] = scaled
    turned = scaled.T
    for q in range(terms):
        for k in range(0, kept, 2):
            @pl.when(counts[q, step] > k)
            def _(q=q, k=k):
                pair = jnp.concatenate([matrices[q, 0, k], matrices[q, 0, k + 1]], axis=1)
                both = jnp.dot(turned, pair, preferred_element_type=jnp.float32)
                acc[slots[q, step, k]] += both[:, :size]
                acc[slots[q, step, k + 1]] += both[:, size:]

    @pl.when(step == pl.num_programs(0) - 1)
    def _():
        stride = owned + ghosts
        copies = []
        for q in range(terms):
            for g in range(ghosts):
                staged[q, :, g * size:(g + 1) * size] = acc[q * stride + owned + g].astype(jnp.bfloat16)
            copies.append(pltpu.make_async_copy(staged.at[q], weights.at[q], went.at[q]))
            copies[-1].start()

        def own(q, carry):
            total = jnp.zeros((columns, columns), jnp.float32)
            for j in range(0, owned, 2):
                exact = jnp.concatenate([acc[q * stride + j], acc[q * stride + j + 1]], axis=1)
                high = exact.astype(jnp.bfloat16)
                low = (exact - high.astype(jnp.float32)).astype(jnp.bfloat16)
                rows = basis[j * size:(j + 2) * size, :]
                total += jnp.dot(high, rows, preferred_element_type=jnp.float32)
                total += jnp.dot(low, rows, preferred_element_type=jnp.float32)
            partial[pl.ds(pl.multiple_of(q * columns, columns), columns), :] = total
            return carry

        lax.fori_loop(0, terms, own, 0)
        for copy in copies:
            copy.wait()


def project(slots, counts, exponents, values, matrices, ghosts):
    terms, owned, kept = slots.shape
    size = matrices.shape[-1]
    columns = values.shape[1]
    wide = ghosts * size
    return pl.pallas_call(
        functools.partial(project_kernel, ghosts),
        grid=(owned,),
        out_shape=(
            jax.ShapeDtypeStruct((terms, columns, wide), jnp.bfloat16),
            jax.ShapeDtypeStruct((terms * columns, columns), jnp.float32),
        ),
        in_specs=[
            SMEM,
            SMEM,
            SMEM,
            pl.BlockSpec((size, columns), lambda b: (b, 0)),
            pl.BlockSpec((terms, 1, kept, size, size), lambda b: (0, b, 0, 0, 0)),
        ],
        out_specs=(HBM, pl.BlockSpec((terms * columns, columns), lambda b: (0, 0))),
        scratch_shapes=[
            pltpu.VMEM((terms * (owned + ghosts) + 1, columns, size), jnp.float32),
            pltpu.VMEM(values.shape, values.dtype),
            pltpu.VMEM((terms, columns, wide), jnp.bfloat16),
            pltpu.SemaphoreType.DMA((terms,)),
        ],
        compiler_params=pltpu.CompilerParams(vmem_limit_bytes=56 * 2**20),
        cost_estimate=pl.CostEstimate(
            flops=2 * matrices.size * columns, bytes_accessed=2 * matrices.size, transcendentals=0
        ),
        name="project",
    )(slots, counts, exponents, values, matrices)


def finish_kernel(share, weights, far, below, above, own, keep, send):
    parity = lax.rem(lax.axis_index("dom"), 2)
    total = own[...]
    start = 0
    for blocks in (far, below, above):
        stop = start + blocks.shape[0]
        total += jnp.dot(weights[:, start:stop], blocks[...], preferred_element_type=jnp.float32)
        start = stop
    halves = total.reshape(-1, 2, share, total.shape[1])
    even = halves[:, 0].reshape(keep.shape)
    odd = halves[:, 1].reshape(keep.shape)
    keep[...] = jnp.where(parity == 0, even, odd)
    send[...] = jnp.where(parity == 0, odd, even)


def finish(weights, far, below, above, own, share, tile):
    rows, wide = weights.shape
    columns = own.shape[1]
    whole = lambda a: pl.BlockSpec(a.shape, lambda t: (0, 0))
    half = jax.ShapeDtypeStruct((rows // 2, columns), jnp.float32)
    return pl.pallas_call(
        functools.partial(finish_kernel, share),
        grid=(rows // tile,),
        out_shape=(half, half),
        in_specs=[
            pl.BlockSpec((tile, wide), lambda t: (t, 0)),
            whole(far),
            whole(below),
            whole(above),
            pl.BlockSpec((tile, columns), lambda t: (t, 0)),
        ],
        out_specs=(pl.BlockSpec((tile // 2, columns), lambda t: (t, 0)),) * 2,
        compiler_params=pltpu.CompilerParams(vmem_limit_bytes=32 * 2**20),
        name="finish",
    )(weights, far, below, above, own)


def on_device(matrices, values, exponents, pattern, block_counts, send_lists, ghost_counts):
    parts = lax.axis_size("dom")
    me = lax.axis_index("dom")
    terms, owned, kept = pattern.shape
    size = matrices.shape[-1]
    lent = send_lists.shape[2]
    row_count, columns = values.shape
    ghosts = parts + 2 * (lent - 1)

    far, after, before = pack(send_lists, exponents, values, size)
    far = lax.all_to_all(far, "dom", split_axis=0, concat_axis=0, tiled=True)
    below = lax.ppermute(after, "dom", [(p, p + 1) for p in range(parts - 1)])
    above = lax.ppermute(before, "dom", [(p + 1, p) for p in range(parts - 1)])

    ghost = pattern - owned
    lender, which = ghost // lent, ghost % lent
    further = parts + which - 1 + jnp.where(lender > me, lent - 1, 0)
    slot = jnp.where(pattern < owned, pattern, owned + jnp.where(which == 0, lender, further))
    slot = slot + (owned + ghosts) * jnp.arange(terms, dtype=jnp.int32)[:, None, None]
    present = jnp.arange(kept)[None, None, :] < block_counts[:, :, None]
    slot = jnp.where(present, slot, terms * (owned + ghosts))

    weights, own = project(slot, block_counts, exponents, values, matrices, ghosts)
    share = terms * columns // parts
    flat = lambda a: a.reshape(-1, columns)
    keep, send = finish(
        weights.reshape(terms * columns, -1), flat(far), flat(below), flat(above), own, share, max(128, 2 * share)
    )
    both = keep + lax.ppermute(send, "dom", [(p, p ^ 1) for p in range(parts)])
    both = both.astype(jnp.bfloat16).reshape(parts // 2, share, columns)
    groups = [list(range(core, parts, 2)) for core in range(2)]
    pieces = lax.all_to_all(both, "dom", split_axis=0, concat_axis=0, tiled=True, axis_index_groups=groups)
    summed = jnp.sum(pieces.astype(jnp.float32), axis=0)
    return summed * (1.0 / math.sqrt(row_count * parts))


def solution(mesh):
    return jax.shard_map(
        on_device,
        mesh=mesh,
        in_specs=(
            P(None, ("group", "dom"), None, None, None),
            P(("group", "dom"), None),
            P(("group", "dom")),
            P(None, ("group", "dom"), None),
            P(None, ("group", "dom")),
            P(("group", "dom"), None, None),
            P(("group", "dom"), None),
        ),
        out_specs=P(("group", "dom"), None),
        check_vma=False,
    )
```

time: 260 us -> 93.8 us (0.36)
  waiting for transfers between devices: 149 us -> 1.9 us
  Pallas kernels: 0 us -> 51.2 us
  local copies, waits for them, and re-layouts: 46.2 us -> 6.01 us
  matrix products: 29 us -> 0 us
  blocking collectives: 0 us -> 20.1 us
  between operations: 13.6 us -> 0.1 us
  other arithmetic: 13.9 us -> 2.14 us
  starting transfers between devices: 7.61 us -> 10.8 us
    all_to_all x1, waiting for transfers between devices: 76.6 us -> 0.01 us  [on_device(): far = lax.all_to_all(far, 'dom', split_axis=0, concat_axis=0, tiled=True)]
    reduce_scatter x1 -> x0, waiting for transfers between devices: 72.5 us -> none  [on_device(): summed = lax.psum_scatter(stacked, 'dom', scatter_dimension=0, tiled=True)]
    pallas_call x0 -> x3, Pallas kernels: none -> 51.2 us  [the longest x1 44.6 us: project(): pl.pallas_call(functools.partial(project_kernel, ghosts), grid=(owned,),...]
    gather x5 -> x0, local copies, waits for them, and re-layouts: 42.7 us -> none  [the longest x4 39.7 us: on_device(): lookup[pattern[which].reshape(-1)]]
    dot_general x4 -> x0, matrix products: 29 us -> none  [on_device(): lax.dot_general(flat_owned, product.reshape(-1, columns), (((0,), (0,)),...]
    all_to_all x0 -> x1, blocking collectives: none -> 20.1 us  [on_device(): lax.all_to_all(both, 'dom', split_axis=0, concat_axis=0, tiled=True, axis...]
    unnamed x5 -> x6, local copies, waits for them, and re-layouts: 0.77 us -> 6.01 us
    concatenate x1 -> x0, other arithmetic: 5.12 us -> none  [on_device(): jnp.concatenate([owned_blocks, incoming.reshape(-1, block_size, columns)]...]
  transfers between devices with their start and end apart: 2 -> 4, of which waited for: 2 -> 1; matrix products, arithmetic and copies ran while one was open for 0% -> 2% of each run, Pallas kernels for 0% -> 48%
where the time goes in v1:
time: 93.8 us; the launch traced here: 92.2 us
  Pallas kernels  51.2 us (55%)
  blocking collectives  20.1 us (21%)
  starting transfers between devices  10.8 us (12%)
  local copies, waits for them, and re-layouts  6.01 us (6%)
  other arithmetic  2.14 us (2%)
  waiting for transfers between devices  1.9 us (2%)
    pallas_call x1, Pallas kernels, project(): pl.pallas_call(functools.partial(project_kernel, ghosts), grid=(owned,),...  44.6 us
    all_to_all x1, blocking collectives, on_device(): lax.all_to_all(both, 'dom', split_axis=0, concat_axis=0, tiled=True, axis...  20.1 us
    all_to_all x1, starting transfers between devices, on_device(): far = lax.all_to_all(far, 'dom', split_axis=0, concat_axis=0, tiled=True)  7.17 us
    unnamed x6, local copies, waits for them, and re-layouts  6.01 us
    pallas_call x1, Pallas kernels, pack(): pl.pallas_call(functools.partial(pack_kernel, parts, size), out_shape=(bl...  3.46 us
    pallas_call x1, Pallas kernels, finish(): pl.pallas_call(functools.partial(finish_kernel, share), grid=(rows // til...  3.06 us
    ppermute x1, starting transfers between devices, on_device(): below = lax.ppermute(after, 'dom', [(p, p + 1) for p in range(parts - 1)])  2.31 us
    ppermute x1, waiting for transfers between devices, on_device(): both = keep + lax.ppermute(send, 'dom', [(p, p ^ 1) for p in range(parts)])  1.9 us
  transfers between devices with their start and end apart: 4, of which 1 were waited for; matrix products, arithmetic and copies ran while one was open for 2% of the time, Pallas kernels for 48%

profile of v1, /device:TPU:0, one launch (start us, length us, event | category | flops | bytes accessed | tf_op | source)
XLA Modules:
  0.0 92.2 jit_solution(13272119740875107058)
XLA Ops:
  0.0 1.4 %copy.10.lists = s32[1,16,4]{2,1,0:T(8,128)} copy(s32[1,16,4]{1,2,0:T(4,128)} %param.12) | data formatting | bytes 512 | tf_op args[5]
  1.4 3.5 %pack.1 = (bf16[16,128,256]{2,1,0:T(8,128)(2,1)}, bf16[3,128,256]{2,1,0:T(8,128)(2,1)}, bf16[3,128,256]{2,1,0:T(8,128)(2,1)}) custom-call(s32[1,16,4]{2,1,0:T(8,128)} %copy.10.lists, s32[24]{0:T(128)} %exponents.3, bf16[3072,256]{1,0:T(8,128)(2,1)} %values.3), custom_call_target="tpu_custom_call" | custom-call | tf_op jit(solution)/shard_map/pack/pallas_call | solution.py:47
  4.8 7.2 %all-to-all-start = ((bf16[16,128,256]{2,1,0:T(8,128)(2,1)}), bf16[16,128,256]{2,1,0:T(8,128)(2,1)S(1)}, u32[]{:S(2)}, u32[]{:S(2)}) async-start(bf16[16,128,256]{2,1,0:T(8,128)(2,1)} %get-tuple-element.13), calls=%async_computation | async-start | bytes 2097152 | tf_op jit(solution)/shard_map/all_to_all | solution.py:193
  12.0 2.3 %collective-permute-start = (bf16[3,128,256]{2,1,0:T(8,128)(2,1)}, bf16[3,128,256]{2,1,0:T(8,128)(2,1)S(1)}, u32[]{:S(2)}, u32[]{:S(2)}) collective-permute-start(bf16[3,128,256]{2,1,0:T(8,128)(2,1)} %get-tuple-element.14), channel_id=1, source_target_pairs={{0,1},{1,2},{2,3},{3,4},{4,5},{5,6},{6,7},{7,8},{8,9},{9,10},{10,1... | collective-permute-start | bytes 589832 | tf_op jit(solution)/shard_map/ppermute | solution.py:194
  14.3 1.3 %collective-permute-start.1 = (bf16[3,128,256]{2,1,0:T(8,128)(2,1)}, bf16[3,128,256]{2,1,0:T(8,128)(2,1)S(1)}, u32[]{:S(2)}, u32[]{:S(2)}) collective-permute-start(bf16[3,128,256]{2,1,0:T(8,128)(2,1)} %get-tuple-element.15), channel_id=1, source_target_pairs={{1,0},{2,1},{3,2},{4,3},{5,4},{6,5},{7,6},{8,7},{9,8},{10,9},{11,1... | collective-permute-start | bytes 589832 | tf_op jit(solution)/shard_map/ppermute | solution.py:195
  15.6 0.8 copy.7
  16.4 1.4 %fusion.1.slots = s32[4,24,6]{2,1,0:T(8,128)} fusion(s32[4,24,6]{2,1,0:T(8,128)S(1)} %copy.7, s32[4]{0:T(128)S(1)} %iota_multiply_fusion, s32[]{:T(128)S(6)} %axis_index.12, s32[4,24]{1,0:T(4,128)} %counts.1), kind=kLoop, calls=%fused_computation.9 | loop fusion | flops 18432 | bytes 5012 | tf_op jit(solution)/shard_map/jit(_where)/select_n | solution.py:203
  17.8 44.6 %project.1 = (bf16[4,256,2816]{2,1,0:T(8,128)(2,1)}, f32[1024,256]{1,0:T(8,128)}) custom-call(s32[4,24,6]{2,1,0:T(8,128)} %fusion.1.slots, s32[4,24]{1,0:T(4,128)} %counts.1, s32[24]{0:T(128)} %exponents.3, bf16[3072,256]{1,0:T(8,128)(2,1)} %values.3, bf16[4,24,6,128,128]{4,3,2,1,0:T(8,128)(2,1)} %matrices.1), custom_call_target="tpu_custom_call" | custom-call | flops 4831838208 | bytes 18874368 | tf_op jit(solution)/shard_map/project/pallas_call | solution.py:117
  62.5 0.0 collective-permute-done
  62.5 0.0 collective-permute-done.1
  62.5 0.0 all-to-all-done
  62.5 0.0 copy-start
  62.5 2.6 %copy-done = bf16[4,256,2816]{2,1,0:T(8,128)(2,1)S(1)} copy-done((bf16[4,256,2816]{2,1,0:T(8,128)(2,1)S(1)}, bf16[4,256,2816]{2,1,0:T(8,128)(2,1)}, u32[]{:S(2)}) %copy-start) | copy-done | bytes 5767192
  65.1 0.0 copy-start.1
  65.1 1.2 %copy-done.1 = f32[1024,256]{1,0:T(8,128)S(1)} copy-done((f32[1024,256]{1,0:T(8,128)S(1)}, f32[1024,256]{1,0:T(8,128)}, u32[]{:S(2)}) %copy-start.1) | copy-done | bytes 1048600
  66.4 3.1 %finish.1 = (f32[512,256]{1,0:T(8,128)S(1)}, f32[512,256]{1,0:T(8,128)S(1)}) custom-call(bf16[1024,2816]{1,0:T(8,128)(2,1)S(1)} %bitcast.5, bf16[2048,256]{1,0:T(8,128)(2,1)S(1)} %bitcast.6, bf16[384,256]{1,0:T(8,128)(2,1)S(1)} %bitcast.7, bf16[384,256]{1,0:T(8,128)(2,1)S(1)} %bitcast.8, f32[1024,256]{1,0:T(8,128)S(1)} %copy-done.1), custom_call_target="tpu_custom_call" | custom-call | tf_op jit(solution)/shard_map/finish/pallas_call | solution.py:166
  69.4 0.1 collective-permute-start.2
  69.5 1.9 %collective-permute-done.2 = f32[512,256]{1,0:T(8,128)S(1)} collective-permute-done((f32[512,256]{1,0:T(8,128)S(1)}, f32[512,256]{1,0:T(8,128)S(1)}, u32[]{:S(2)}, u32[]{:S(2)}) %collective-permute-start.2) | collective-permute-done | bytes 524320 | tf_op jit(solution)/shard_map/ppermute | solution.py:211
  71.4 0.1 add_convert_fusion
  71.5 20.1 %all_to_all.10 = bf16[8,64,256]{2,1,0:T(8,128)(2,1)S(1)} all-to-all(bf16[8,64,256]{2,1,0:T(8,128)(2,1)S(1)} %bitcast.9), channel_id=1, replica_groups={{0,2,4,6,8,10,12,14},{1,3,5,7,9,11,13,15},{16,18,20,22,24,26,28,30},{17..., dimensions={0} | all-to-all | bytes 524288 | tf_op jit(solution)/shard_map/all_to_all | solution.py:214
  91.6 0.6 broadcast_multiply_fusion
  (2 shorter events, 0.0 us)
Async XLA Ops:
  4.8 57.7 %all-to-all-start = ((bf16[16,128,256]{2,1,0:T(8,128)(2,1)}), bf16[16,128,256]{2,1,0:T(8,128)(2,1)S(1)}, u32[]{:S(2)}, u32[]{:S(2)}) async-start(bf16[16,128,256]{2,1,0:T(8,128)(2,1)} %get-tuple-element.13), calls=%async_computation | async-start | bytes 2097152 | tf_op jit(solution)/shard_map/all_to_all | solution.py:193
  12.0 50.5 %collective-permute-start = (bf16[3,128,256]{2,1,0:T(8,128)(2,1)}, bf16[3,128,256]{2,1,0:T(8,128)(2,1)S(1)}, u32[]{:S(2)}, u32[]{:S(2)}) collective-permute-start(bf16[3,128,256]{2,1,0:T(8,128)(2,1)} %get-tuple-element.14), channel_id=1, source_target_pairs={{0,1},{1,2},{2,3},{3,4},{4,5},{5,6},{6,7},{7,8},{8,9},{9,10},{10,1... | collective-permute-start | bytes 589832 | tf_op jit(solution)/shard_map/ppermute | solution.py:194
  14.3 48.2 %collective-permute-start.1 = (bf16[3,128,256]{2,1,0:T(8,128)(2,1)}, bf16[3,128,256]{2,1,0:T(8,128)(2,1)S(1)}, u32[]{:S(2)}, u32[]{:S(2)}) collective-permute-start(bf16[3,128,256]{2,1,0:T(8,128)(2,1)} %get-tuple-element.15), channel_id=1, source_target_pairs={{1,0},{2,1},{3,2},{4,3},{5,4},{6,5},{7,6},{8,7},{9,8},{10,9},{11,1... | collective-permute-start | bytes 589832 | tf_op jit(solution)/shard_map/ppermute | solution.py:195
  62.5 2.6 %copy-start = (bf16[4,256,2816]{2,1,0:T(8,128)(2,1)S(1)}, bf16[4,256,2816]{2,1,0:T(8,128)(2,1)}, u32[]{:S(2)}) copy-start(bf16[4,256,2816]{2,1,0:T(8,128)(2,1)} %get-tuple-element.12) | copy-start | bytes 17301508
  65.1 1.2 %copy-start.1 = (f32[1024,256]{1,0:T(8,128)S(1)}, f32[1024,256]{1,0:T(8,128)}, u32[]{:S(2)}) copy-start(f32[1024,256]{1,0:T(8,128)} %get-tuple-element.16.own) | copy-start | bytes 3145732
  69.4 2.0 %collective-permute-start.2 = (f32[512,256]{1,0:T(8,128)S(1)}, f32[512,256]{1,0:T(8,128)S(1)}, u32[]{:S(2)}, u32[]{:S(2)}) collective-permute-start(f32[512,256]{1,0:T(8,128)S(1)} %get-tuple-element.18), channel_id=1, source_target_pairs={{0,1},{1,0},{2,3},{3,2},{4,5},{5,4},{6,7},{7,6},{8,9},{9,8},{10,11... | collective-permute-start | bytes 1572872 | tf_op jit(solution)/shard_map/ppermute | solution.py:211

commit v2 on v0

v2 whole, which is shorter than its diff:
```python
import functools
import math

import jax
import jax.numpy as jnp
from jax import lax
from jax.experimental import pallas as pl
from jax.experimental.pallas import tpu as pltpu
from jax.sharding import PartitionSpec as P

SMEM = pl.BlockSpec(memory_space=pltpu.SMEM)
VMEM = pl.BlockSpec(memory_space=pltpu.VMEM)
HBM = pl.BlockSpec(memory_space=pl.ANY)


def power_of_two(exponent):
    return (lax.shift_left(jnp.int32(1), exponent + 2).astype(jnp.float32) * 0.25).astype(jnp.bfloat16)


def pack_kernel(parts, size, lists, exponents, values, far, after, before):
    me = lax.axis_index("dom")
    lent = lists.shape[1]
    upper = jnp.minimum(me + 1, parts - 1)
    lower = jnp.maximum(me - 1, 0)

    def lend(block, out, n):
        rows = pl.ds(pl.multiple_of(block * size, size), size)
        out[n] = values[rows, :] * power_of_two(exponents[block])

    for p in range(parts):
        lend(lists[0, 0, p], far, p)
    for g in range(1, lent):
        lend(lists[0, g, upper], after, g - 1)
        lend(lists[0, g, lower], before, g - 1)


def pack(lists, exponents, values, size):
    lent, parts = lists.shape[1:]
    columns = values.shape[1]
    block = lambda n: jax.ShapeDtypeStruct((n, size, columns), values.dtype)
    return pl.pallas_call(
        functools.partial(pack_kernel, parts, size),
        out_shape=(block(parts), block(lent - 1), block(lent - 1)),
        in_specs=[SMEM, SMEM, VMEM],
        out_specs=(VMEM, VMEM, VMEM),
        name="pack",
    )(lists, exponents, values)


def project_kernel(
    parts, lent, pattern, counts, exponents, values, matrices, weights, partial,
    acc, basis, high, low, ring, came, terms_of, slots_of,
):
    me = lax.axis_index("dom")
    kept, terms, owned = pattern.shape
    depth = ring.shape[0]
    size = ring.shape[-1]
    columns = values.shape[1]
    ghosts = parts + 2 * (lent - 1)
    steps = owned // 2

    def fetch(step, place):
        return pltpu.make_async_copy(matrices.at[:, pl.ds(2 * step, 2)], ring.at[place], came.at[place])

    for step in range(depth):
        fetch(step, step).start()

    def clear(n, carry):
        acc[n] = jnp.zeros(acc.shape[1:], acc.dtype)
        return carry

    lax.fori_loop(0, acc.shape[0], clear, 0)

    def scale(n, carry):
        rows = pl.ds(pl.multiple_of(n * size, size), size)
        basis[n] = values[rows, :] * power_of_two(exponents[n])
        return carry

    lax.fori_loop(0, owned, scale, 0)
    basis[owned] = jnp.zeros(basis.shape[1:], basis.dtype)
    partial[...] = jnp.zeros(partial.shape, partial.dtype)

    def body(step, carry):
        place = lax.rem(step, depth)
        fetch(step, place).wait()
        rows = jnp.concatenate([basis[2 * step], basis[2 * step + 1]], axis=0)
        turned = rows.T
        listed = []
        for sub in range(2):
            b = 2 * step + sub
            found = jnp.int32(0)
            for q in range(terms):
                count = counts[q, b]
                before = found
                tables = []
                for k in range(kept):
                    slot = pattern[k, q, b]
                    present = count > k
                    tables.append(basis[jnp.where(present & (slot < owned), slot, owned)])
                    terms_of[sub, found] = q
                    slots_of[sub, found] = k
                    found += (present & (slot >= owned)).astype(jnp.int32)
                left = jnp.concatenate([ring[place, q, sub, k] for k in range(kept)], axis=1)
                exact = jnp.dot(left, jnp.concatenate(tables, axis=0), preferred_element_type=jnp.float32)
                upper = exact.astype(jnp.bfloat16)
                rest = (exact - upper.astype(jnp.float32)) * (found > before).astype(jnp.float32)
                high[q, sub * size:(sub + 1) * size, :] = upper
                low[q, sub * size:(sub + 1) * size, :] = rest.astype(jnp.bfloat16)
            listed.append(found)
        for q in range(terms):
            rows = slice(q * columns, (q + 1) * columns)
            partial[rows, :] += jnp.dot(turned, high[q], preferred_element_type=jnp.float32) + jnp.dot(
                turned, low[q], preferred_element_type=jnp.float32
            )
        for sub in range(2):
            b = 2 * step + sub
            left = turned[:, sub * size:(sub + 1) * size]

            def ghost(n, carry, sub=sub, b=b, left=left):
                def take(n):
                    real = n < listed[sub]
                    q = jnp.where(real, terms_of[sub, n], 0)
                    k = jnp.where(real, slots_of[sub, n], 0)
                    slot = pattern[k, q, b] - owned
                    lender, which = lax.div(slot, lent), lax.rem(slot, lent)
                    further = parts + which - 1 + jnp.where(lender > me, lent - 1, 0)
                    target = q * ghosts + jnp.where(which == 0, lender, further)
                    return ring[place, q, sub, k], jnp.where(real, target, terms * ghosts)

                first, first_target = take(2 * n)
                second, second_target = take(2 * n + 1)
                both = jnp.dot(left, jnp.concatenate([first, second], axis=1), preferred_element_type=jnp.float32)
                acc[first_target] += both[:, :size]
                acc[second_target] += both[:, size:]
                return carry

            lax.fori_loop(0, lax.div(listed[sub] + 1, 2), ghost, 0)

        @pl.when(step + depth < steps)
        def _():
            fetch(step + depth, place).start()

        return carry

    lax.fori_loop(0, steps, body, 0)

    def settle(q, carry):
        rows = pl.ds(pl.multiple_of(q * columns, columns), columns)
        for g in range(ghosts):
            weights[rows, g * size:(g + 1) * size] = acc[q * ghosts + g].astype(jnp.bfloat16)
        return carry

    lax.fori_loop(0, terms, settle, 0)


def project(pattern, counts, exponents, values, matrices, parts, lent):
    kept, terms, owned = pattern.shape
    size = matrices.shape[-1]
    columns = values.shape[1]
    ghosts = parts + 2 * (lent - 1)
    depth = 3
    scratch = [
        ((terms * ghosts + 1, columns, size), jnp.float32),
        ((owned + 1, size, columns), jnp.bfloat16),
        ((terms, 2 * size, columns), jnp.bfloat16),
        ((terms, 2 * size, columns), jnp.bfloat16),
        ((depth, terms, 2, kept, size, size), jnp.bfloat16),
    ]
    outs = [((terms * columns, ghosts * size), jnp.bfloat16), ((terms * columns, columns), jnp.float32)]
    needed = sum(math.prod(shape) * jnp.dtype(dtype).itemsize for shape, dtype in scratch + outs + [(values.shape, jnp.bfloat16)])
    return pl.pallas_call(
        functools.partial(project_kernel, parts, lent),
        out_shape=tuple(jax.ShapeDtypeStruct(*out) for out in outs),
        in_specs=[SMEM, SMEM, SMEM, VMEM, HBM],
        out_specs=(VMEM, VMEM),
        scratch_shapes=[pltpu.VMEM(shape, dtype) for shape, dtype in scratch] + [
            pltpu.SemaphoreType.DMA((depth,)),
            pltpu.SMEM((2, terms * kept + 1), jnp.int32),
            pltpu.SMEM((2, terms * kept + 1), jnp.int32),
        ],
        compiler_params=pltpu.CompilerParams(vmem_limit_bytes=needed + 4 * 2**20),
        cost_estimate=pl.CostEstimate(
            flops=2 * matrices.size * columns, bytes_accessed=2 * matrices.size, transcendentals=0
        ),
        name="project",
    )(pattern, counts, exponents, values, matrices)


def finish_kernel(share, weights, far, below, above, own, keep, send):
    parity = lax.rem(lax.axis_index("dom"), 2)
    columns = own.shape[1]
    tile = max(columns, 2 * share)
    for first in range(0, own.shape[0], tile):
        rows = slice(first, first + tile)
        total = own[rows, :]
        start = 0
        for blocks in (far, below, above):
            stop = start + blocks.shape[0]
            total += jnp.dot(weights[rows, start:stop], blocks[...], preferred_element_type=jnp.float32)
            start = stop
        halves = total.reshape(-1, 2, share, columns)
        even = halves[:, 0].reshape(-1, columns)
        odd = halves[:, 1].reshape(-1, columns)
        half = slice(first // 2, (first + tile) // 2)
        keep[half, :] = jnp.where(parity == 0, even, odd)
        send[half, :] = jnp.where(parity == 0, odd, even)


def finish(weights, far, below, above, own, share):
    half = jax.ShapeDtypeStruct((own.shape[0] // 2, own.shape[1]), jnp.float32)
    return pl.pallas_call(
        functools.partial(finish_kernel, share),
        out_shape=(half, half),
        in_specs=[VMEM] * 5,
        out_specs=(VMEM, VMEM),
        compiler_params=pltpu.CompilerParams(vmem_limit_bytes=24 * 2**20),
        name="finish",
    )(weights, far, below, above, own)


def on_device(matrices, values, exponents, pattern, block_counts, send_lists, ghost_counts):
    parts = lax.axis_size("dom")
    terms = pattern.shape[0]
    size = matrices.shape[-1]
    lent = send_lists.shape[2]
    row_count, columns = values.shape

    far, after, before = pack(jnp.transpose(send_lists, (0, 2, 1)), exponents, values, size)
    far = lax.all_to_all(far, "dom", split_axis=0, concat_axis=0, tiled=True)
    below = lax.ppermute(after, "dom", [(p, p + 1) for p in range(parts - 1)])
    above = lax.ppermute(before, "dom", [(p + 1, p) for p in range(parts - 1)])

    weights, own = project(
        jnp.transpose(pattern, (2, 0, 1)), block_counts, exponents, values, matrices, parts, lent
    )
    share = terms * columns // parts
    flat = lambda a: a.reshape(-1, columns)
    keep, send = finish(weights, flat(far), flat(below), flat(above), own, share)
    both = keep + lax.ppermute(send, "dom", [(p, p ^ 1) for p in range(parts)])
    both = both.astype(jnp.bfloat16).reshape(parts // 2, share, columns)
    groups = [list(range(core, parts, 2)) for core in range(2)]
    pieces = lax.all_to_all(both, "dom", split_axis=0, concat_axis=0, tiled=True, axis_index_groups=groups)
    summed = jnp.sum(pieces.astype(jnp.float32), axis=0)
    return summed * (1.0 / math.sqrt(row_count * parts))


def solution(mesh):
    return jax.shard_map(
        on_device,
        mesh=mesh,
        in_specs=(
            P(None, ("group", "dom"), None, None, None),
            P(("group", "dom"), None),
            P(("group", "dom")),
            P(None, ("group", "dom"), None),
            P(None, ("group", "dom")),
            P(("group", "dom"), None, None),
            P(("group", "dom"), None),
        ),
        out_specs=P(("group", "dom"), None),
        check_vma=False,
    )
```

time: 260 us -> 68.2 us (0.26)
  waiting for transfers between devices: 149 us -> 1.54 us
  local copies, waits for them, and re-layouts: 46.2 us -> 8.54 us
  matrix products: 29 us -> 0 us
  Pallas kernels: 0 us -> 21.3 us
  blocking collectives: 0 us -> 15.5 us
  between operations: 13.6 us -> 0.08 us
  other arithmetic: 13.9 us -> 0.75 us
  starting transfers between devices: 7.61 us -> 19.2 us
    all_to_all x1, waiting for transfers between devices: 76.6 us -> 0.01 us  [on_device(): far = lax.all_to_all(far, 'dom', split_axis=0, concat_axis=0, tiled=True)]
    reduce_scatter x1 -> x0, waiting for transfers between devices: 72.5 us -> none  [on_device(): summed = lax.psum_scatter(stacked, 'dom', scatter_dimension=0, tiled=True)]
    gather x5 -> x0, local copies, waits for them, and re-layouts: 42.7 us -> none  [the longest x4 39.7 us: on_device(): lookup[pattern[which].reshape(-1)]]
    dot_general x4 -> x0, matrix products: 29 us -> none  [on_device(): lax.dot_general(flat_owned, product.reshape(-1, columns), (((0,), (0,)),...]
    pallas_call x0 -> x3, Pallas kernels: none -> 21.3 us  [the longest x1 16.9 us: project(): pl.pallas_call(functools.partial(project_kernel, parts, lent), out_shape=...]
    all_to_all x0 -> x1, blocking collectives: none -> 15.5 us  [on_device(): lax.all_to_all(both, 'dom', split_axis=0, concat_axis=0, tiled=True, axis...]
    ppermute x0 -> x3, starting transfers between devices: none -> 11.9 us  [the longest x1 8.25 us: on_device(): both = keep + lax.ppermute(send, 'dom', [(p, p ^ 1) for p in range(parts)])]
    unnamed x5 -> x12, local copies, waits for them, and re-layouts: 0.77 us -> 8.54 us
  transfers between devices with their start and end apart: 2 -> 4, of which waited for: 2 -> 1; matrix products, arithmetic and copies ran while one was open for 0% -> 0% of each run, Pallas kernels for 0% -> 25%
where the time goes in v2:
time: 68.2 us; the launch traced here: 67 us
  Pallas kernels  21.3 us (31%)
  starting transfers between devices  19.2 us (28%)
  blocking collectives  15.5 us (23%)
  local copies, waits for them, and re-layouts  8.54 us (13%)
  waiting for transfers between devices  1.54 us (2%)
  other arithmetic  0.75 us (1%)
    pallas_call x1, Pallas kernels, project(): pl.pallas_call(functools.partial(project_kernel, parts, lent), out_shape=...  16.9 us
    all_to_all x1, blocking collectives, on_device(): lax.all_to_all(both, 'dom', split_axis=0, concat_axis=0, tiled=True, axis...  15.5 us
    unnamed x12, local copies, waits for them, and re-layouts  8.54 us
    ppermute x1, starting transfers between devices, on_device(): both = keep + lax.ppermute(send, 'dom', [(p, p ^ 1) for p in range(parts)])  8.25 us
    all_to_all x1, starting transfers between devices, on_device(): far = lax.all_to_all(far, 'dom', split_axis=0, concat_axis=0, tiled=True)  7.39 us
    pallas_call x1, Pallas kernels, pack(): pl.pallas_call(functools.partial(pack_kernel, parts, size), out_shape=(bl...  2.67 us
    ppermute x1, starting transfers between devices, on_device(): below = lax.ppermute(after, 'dom', [(p, p + 1) for p in range(parts - 1)])  2.31 us
    pallas_call x1, Pallas kernels, finish(): pl.pallas_call(functools.partial(finish_kernel, share), out_shape=(half,...  1.79 us
  transfers between devices with their start and end apart: 4, of which 1 were waited for; matrix products, arithmetic and copies ran while one was open for 0% of the time, Pallas kernels for 25%

profile of v2, /device:TPU:0, one launch (start us, length us, event | category | flops | bytes accessed | tf_op | source)
XLA Modules:
  0.0 67.0 jit_solution(5843314719930272678)
XLA Ops:
  0.0 2.7 %pack.1 = (bf16[16,128,256]{2,1,0:T(8,128)(2,1)}, bf16[3,128,256]{2,1,0:T(8,128)(2,1)}, bf16[3,128,256]{2,1,0:T(8,128)(2,1)}) custom-call(s32[1,4,16]{2,1,0:T(4,128)} %bitcast.11, s32[24]{0:T(128)} %exponents.3, bf16[3072,256]{1,0:T(8,128)(2,1)} %values.3), custom_call_target="tpu_custom_call" | custom-call | tf_op jit(solution)/shard_map/pack/pallas_call | solution.py:41
  2.7 7.4 %all-to-all-start = ((bf16[16,128,256]{2,1,0:T(8,128)(2,1)}), bf16[16,128,256]{2,1,0:T(8,128)(2,1)S(1)}, u32[]{:S(2)}, u32[]{:S(2)}) async-start(bf16[16,128,256]{2,1,0:T(8,128)(2,1)} %get-tuple-element.13), calls=%async_computation | async-start | bytes 2097152 | tf_op jit(solution)/shard_map/all_to_all | solution.py:229
  10.1 2.3 %collective-permute-start = (bf16[3,128,256]{2,1,0:T(8,128)(2,1)}, bf16[3,128,256]{2,1,0:T(8,128)(2,1)S(1)}, u32[]{:S(2)}, u32[]{:S(2)}) collective-permute-start(bf16[3,128,256]{2,1,0:T(8,128)(2,1)} %get-tuple-element.14), channel_id=1, source_target_pairs={{0,1},{1,2},{2,3},{3,4},{4,5},{5,6},{6,7},{7,8},{8,9},{9,10},{10,1... | collective-permute-start | bytes 589832 | tf_op jit(solution)/shard_map/ppermute | solution.py:230
  12.4 1.3 %collective-permute-start.1 = (bf16[3,128,256]{2,1,0:T(8,128)(2,1)}, bf16[3,128,256]{2,1,0:T(8,128)(2,1)S(1)}, u32[]{:S(2)}, u32[]{:S(2)}) collective-permute-start(bf16[3,128,256]{2,1,0:T(8,128)(2,1)} %get-tuple-element.15), channel_id=1, source_target_pairs={{1,0},{2,1},{3,2},{4,3},{5,4},{6,5},{7,6},{8,7},{9,8},{10,9},{11,1... | collective-permute-start | bytes 589832 | tf_op jit(solution)/shard_map/ppermute | solution.py:231
  13.7 0.0 copy-start
  13.7 1.4 %copy-done = bf16[3072,256]{1,0:T(8,128)(2,1)S(1)} copy-done((bf16[3072,256]{1,0:T(8,128)(2,1)S(1)}, bf16[3072,256]{1,0:T(8,128)(2,1)}, u32[]{:S(2)}) %copy-start) | copy-done | bytes 1572888
  15.1 0.0 copy-start.3
  15.1 0.7 %copy-done.3 = s32[4,24,6]{1,0,2:T(4,128)S(1)} copy-done((s32[4,24,6]{1,0,2:T(4,128)S(1)}, s32[4,24,6]{1,0,2:T(4,128)}, u32[]{:S(2)}) %copy-start.3) | copy-done | bytes 2328
  15.8 0.0 copy-start.4
  15.8 0.7 copy-done.4
  16.5 0.0 copy-start.5
  16.5 0.7 %copy-done.5 = s32[4,24]{1,0:T(4,128)S(1)} copy-done((s32[4,24]{1,0:T(4,128)S(1)}, s32[4,24]{1,0:T(4,128)}, u32[]{:S(2)}) %copy-start.5) | copy-done | bytes 408
  17.1 16.9 %project.1 = (bf16[1024,2816]{1,0:T(8,128)(2,1)S(1)}, f32[1024,256]{1,0:T(8,128)S(1)}) custom-call(s32[6,4,24]{2,1,0:T(4,128)S(1)} %bitcast.9, s32[4,24]{1,0:T(4,128)S(1)} %copy-done.5, s32[24]{0:T(128)S(1)} %copy-done.4, bf16[3072,256]{1,0:T(8,128)(2,1)S(1)} %copy-done, bf16[4,24,6,128,128]{4,3,2,1,0:T(8,128)(2,1)} %matrices.1), custom_call_target="tpu_custom_call" | custom-call | flops 4831838208 | bytes 18874368 | tf_op jit(solution)/shard_map/project/pallas_call | solution.py:171
  34.0 0.0 copy-start.1
  34.0 2.5 %copy-done.1 = bf16[1024,2816]{1,0:T(8,128)(2,1)} copy-done((bf16[1024,2816]{1,0:T(8,128)(2,1)}, bf16[1024,2816]{1,0:T(8,128)(2,1)S(1)}, u32[]{:S(2)}) %copy-start.1) | copy-done | bytes 5767192
  36.5 0.0 collective-permute-done
  36.5 0.0 collective-permute-done.1
  36.5 0.0 all-to-all-done
  36.5 0.0 copy-start.2
  36.5 2.6 %copy-done.2 = bf16[1024,2816]{1,0:T(8,128)(2,1)S(1)} copy-done((bf16[1024,2816]{1,0:T(8,128)(2,1)S(1)}, bf16[1024,2816]{1,0:T(8,128)(2,1)}, u32[]{:S(2)}) %copy-start.2) | copy-done | bytes 5767192
  39.2 1.8 %finish.1 = (f32[512,256]{1,0:T(8,128)S(1)}, f32[512,256]{1,0:T(8,128)S(1)}) custom-call(bf16[1024,2816]{1,0:T(8,128)(2,1)S(1)} %copy-done.2, bf16[2048,256]{1,0:T(8,128)(2,1)S(1)} %bitcast.6, bf16[384,256]{1,0:T(8,128)(2,1)S(1)} %bitcast.7, bf16[384,256]{1,0:T(8,128)(2,1)S(1)} %bitcast.8, f32[1024,256]{1,0:T(8,128)S(1)} %get-tuple-element.16.own), custom_call_target="tpu_custom_call" | custom-call | tf_op jit(solution)/shard_map/finish/pallas_call | solution.py:211
  41.0 8.2 %collective-permute-start.2 = (f32[512,256]{1,0:T(8,128)S(1)}, f32[512,256]{1,0:T(8,128)S(1)}, u32[]{:S(2)}, u32[]{:S(2)}) collective-permute-start(f32[512,256]{1,0:T(8,128)S(1)} %get-tuple-element.18), channel_id=1, source_target_pairs={{0,1},{1,0},{2,3},{3,2},{4,5},{5,4},{6,7},{7,6},{8,9},{9,8},{10,11... | collective-permute-start | bytes 1572872 | tf_op jit(solution)/shard_map/ppermute | solution.py:239
  49.2 1.5 %collective-permute-done.2 = f32[512,256]{1,0:T(8,128)S(1)} collective-permute-done((f32[512,256]{1,0:T(8,128)S(1)}, f32[512,256]{1,0:T(8,128)S(1)}, u32[]{:S(2)}, u32[]{:S(2)}) %collective-permute-start.2) | collective-permute-done | bytes 524320 | tf_op jit(solution)/shard_map/ppermute | solution.py:239
  50.7 0.1 add_convert_fusion
  50.8 15.5 %all_to_all.10 = bf16[8,64,256]{2,1,0:T(8,128)(2,1)S(1)} all-to-all(bf16[8,64,256]{2,1,0:T(8,128)(2,1)S(1)} %bitcast.10), channel_id=1, replica_groups={{0,2,4,6,8,10,12,14},{1,3,5,7,9,11,13,15},{16,18,20,22,24,26,28,30},{17..., dimensions={0} | all-to-all | bytes 524288 | tf_op jit(solution)/shard_map/all_to_all | solution.py:242
  66.4 0.6 broadcast_multiply_fusion
  (1 shorter events, 0.0 us)
Async XLA Ops:
  2.7 33.8 %all-to-all-start = ((bf16[16,128,256]{2,1,0:T(8,128)(2,1)}), bf16[16,128,256]{2,1,0:T(8,128)(2,1)S(1)}, u32[]{:S(2)}, u32[]{:S(2)}) async-start(bf16[16,128,256]{2,1,0:T(8,128)(2,1)} %get-tuple-element.13), calls=%async_computation | async-start | bytes 2097152 | tf_op jit(solution)/shard_map/all_to_all | solution.py:229
  10.1 26.4 %collective-permute-start = (bf16[3,128,256]{2,1,0:T(8,128)(2,1)}, bf16[3,128,256]{2,1,0:T(8,128)(2,1)S(1)}, u32[]{:S(2)}, u32[]{:S(2)}) collective-permute-start(bf16[3,128,256]{2,1,0:T(8,128)(2,1)} %get-tuple-element.14), channel_id=1, source_target_pairs={{0,1},{1,2},{2,3},{3,4},{4,5},{5,6},{6,7},{7,8},{8,9},{9,10},{10,1... | collective-permute-start | bytes 589832 | tf_op jit(solution)/shard_map/ppermute | solution.py:230
  12.4 24.1 %collective-permute-start.1 = (bf16[3,128,256]{2,1,0:T(8,128)(2,1)}, bf16[3,128,256]{2,1,0:T(8,128)(2,1)S(1)}, u32[]{:S(2)}, u32[]{:S(2)}) collective-permute-start(bf16[3,128,256]{2,1,0:T(8,128)(2,1)} %get-tuple-element.15), channel_id=1, source_target_pairs={{1,0},{2,1},{3,2},{4,3},{5,4},{6,5},{7,6},{8,7},{9,8},{10,9},{11,1... | collective-permute-start | bytes 589832 | tf_op jit(solution)/shard_map/ppermute | solution.py:231
  13.7 1.4 %copy-start = (bf16[3072,256]{1,0:T(8,128)(2,1)S(1)}, bf16[3072,256]{1,0:T(8,128)(2,1)}, u32[]{:S(2)}) copy-start(bf16[3072,256]{1,0:T(8,128)(2,1)} %values.3) | copy-start | bytes 4718596
  15.1 0.7 %copy-start.3 = (s32[4,24,6]{1,0,2:T(4,128)S(1)}, s32[4,24,6]{1,0,2:T(4,128)}, u32[]{:S(2)}) copy-start(s32[4,24,6]{1,0,2:T(4,128)} %param.10) | copy-start | bytes 6916
  15.8 0.7 copy-start.4
  16.5 0.7 %copy-start.5 = (s32[4,24]{1,0:T(4,128)S(1)}, s32[4,24]{1,0:T(4,128)}, u32[]{:S(2)}) copy-start(s32[4,24]{1,0:T(4,128)} %counts.1) | copy-start | bytes 1156
  34.0 2.5 %copy-start.1 = (bf16[1024,2816]{1,0:T(8,128)(2,1)}, bf16[1024,2816]{1,0:T(8,128)(2,1)S(1)}, u32[]{:S(2)}) copy-start(bf16[1024,2816]{1,0:T(8,128)(2,1)S(1)} %get-tuple-element.12.weights) | copy-start | bytes 17301508
  36.5 2.6 %copy-start.2 = (bf16[1024,2816]{1,0:T(8,128)(2,1)S(1)}, bf16[1024,2816]{1,0:T(8,128)(2,1)}, u32[]{:S(2)}) copy-start(bf16[1024,2816]{1,0:T(8,128)(2,1)} %copy-done.1) | copy-start | bytes 17301508
  41.0 9.8 %collective-permute-start.2 = (f32[512,256]{1,0:T(8,128)S(1)}, f32[512,256]{1,0:T(8,128)S(1)}, u32[]{:S(2)}, u32[]{:S(2)}) collective-permute-start(f32[512,256]{1,0:T(8,128)S(1)} %get-tuple-element.18), channel_id=1, source_target_pairs={{0,1},{1,0},{2,3},{3,2},{4,5},{5,4},{6,7},{7,6},{8,9},{9,8},{10,11... | collective-permute-start | bytes 1572872 | tf_op jit(solution)/shard_map/ppermute | solution.py:239

commit v3 on v2

v3 whole, which is shorter than its diff:
```python
import functools
import math

import jax
import jax.numpy as jnp
from jax import lax
from jax.experimental import pallas as pl
from jax.experimental.pallas import tpu as pltpu
from jax.sharding import PartitionSpec as P

SMEM = pl.BlockSpec(memory_space=pltpu.SMEM)
VMEM = pl.BlockSpec(memory_space=pltpu.VMEM)
ANY = pl.BlockSpec(memory_space=pl.ANY)


def power_of_two(exponent):
    return (lax.shift_left(jnp.int32(1), exponent + 2).astype(jnp.float32) * 0.25).astype(jnp.bfloat16)


def pack_kernel(parts, size, lists, exponents, values, far, after, before):
    me = lax.axis_index("dom")
    lent = lists.shape[1]
    upper = jnp.minimum(me + 1, parts - 1)
    lower = jnp.maximum(me - 1, 0)

    def lend(block, out, n):
        rows = pl.ds(pl.multiple_of(block * size, size), size)
        out[n] = values[rows, :] * power_of_two(exponents[block])

    for p in range(parts):
        lend(lists[0, 0, p], far, p)
    for g in range(1, lent):
        lend(lists[0, g, upper], after, g - 1)
        lend(lists[0, g, lower], before, g - 1)


def pack(lists, exponents, values, size):
    lent, parts = lists.shape[1:]
    columns = values.shape[1]
    block = lambda n: jax.ShapeDtypeStruct((n, size, columns), values.dtype)
    return pl.pallas_call(
        functools.partial(pack_kernel, parts, size),
        out_shape=(block(parts), block(lent - 1), block(lent - 1)),
        in_specs=[SMEM, SMEM, VMEM],
        out_specs=(VMEM, VMEM, VMEM),
        name="pack",
    )(lists, exponents, values)


def project_kernel(parts, lent, middle, wide, pattern_in, counts_in, exponents_in, values_in, matrices, *refs):
    kept, terms, owned = pattern_in.shape
    weights, partial = refs[:2]
    (acc, basis, turned, split, held, staged, values, pattern, counts, own_table, ghost_table,
     own_slots, ghost_slots, exponents, listed, came, read, moved, went) = refs[2:]
    me = lax.axis_index("dom")
    size = held.shape[-1]
    columns = values.shape[1]
    ghosts = parts + 2 * (lent - 1)
    trash = terms * ghosts
    steps = owned // 2

    def fetch(step):
        pair = pl.ds(2 * step, 2)
        return pltpu.make_async_copy(matrices.at[:, pair], held.at[:, pair], came.at[step])

    reads = [
        pltpu.make_async_copy(source, target, read.at[n])
        for n, (source, target) in enumerate(
            [(pattern_in, pattern), (counts_in, counts), (exponents_in, exponents), (values_in, values)]
        )
    ]
    for copy in reads:
        copy.start()
    for step in range(2):
        fetch(step).start()

    def clear(n, carry):
        acc[n] = jnp.zeros(acc.shape[1:], acc.dtype)
        return carry

    lax.fori_loop(0, acc.shape[0], clear, 0)
    basis[owned] = jnp.zeros(basis.shape[1:], basis.dtype)
    partial[...] = jnp.zeros(partial.shape, partial.dtype)
    reads[0].wait()
    reads[1].wait()

    slot = pattern[...]
    k, q, b = (lax.broadcasted_iota(jnp.int32, slot.shape, n) for n in range(3))
    present = k < counts[...][None]
    ghost = present & (slot >= owned)
    lender, which = (slot - owned) // lent, (slot - owned) % lent
    further = parts + which - 1 + jnp.where(lender > me, lent - 1, 0)
    target = q * ghosts + jnp.where(which == 0, lender, further)
    some = jnp.max(ghost.astype(jnp.int32), axis=0, keepdims=True)
    own_table[...] = jnp.where(present & (slot < owned), slot, owned) + jnp.where(k == 0, 256 * some, 0)
    ghost_table[...] = jnp.where(ghost, (1 << 30) + (target << 16) + (b << 8) + (q << 4) + k, 0)
    moves = [
        pltpu.make_async_copy(own_table, own_slots, moved.at[0]),
        pltpu.make_async_copy(ghost_table, ghost_slots, moved.at[1]),
    ]
    for copy in moves:
        copy.start()
    for step in range(2, steps):
        fetch(step).start()
    for copy in moves + reads[2:]:
        copy.wait()

    def prepare(n, found):
        rows = pl.ds(pl.multiple_of(n * size, size), size)
        scaled = values[rows, :] * power_of_two(exponents[n])
        basis[n] = scaled
        turned[n] = scaled.T
        for q in range(terms):
            for k in range(kept):
                word = ghost_slots[k, q, n]
                listed[found] = word
                found += lax.shift_right_logical(word, 30)
        return found

    found = lax.fori_loop(0, owned, prepare, jnp.int32(0))
    for n in range(2 * wide):
        listed[found + n] = trash << 16

    def multiply(step):
        slot = lax.rem(step, 2)
        for sub in range(2):
            b = 2 * step + sub
            for q in range(terms):
                words = [own_slots[k, q, b] for k in range(kept)]
                mixed = lax.shift_right_logical(words[0], 8)
                words[0] = words[0] & 255
                left = jnp.concatenate([held[q, b, k] for k in range(kept)], axis=1)
                table = jnp.concatenate([basis[word] for word in words], axis=0)
                exact = jnp.dot(left, table, preferred_element_type=jnp.float32)
                upper = exact.astype(jnp.bfloat16)
                rest = (exact - upper.astype(jnp.float32)) * mixed.astype(jnp.float32)
                split[slot, q, sub * size:(sub + 1) * size, :] = upper
                split[slot, q, (2 + sub) * size:(3 + sub) * size, :] = rest.astype(jnp.bfloat16)

    def gather(step):
        slot = lax.rem(step, 2)
        left = jnp.concatenate([turned[2 * step], turned[2 * step + 1]] * 2, axis=1)
        for q in range(terms):
            rows = slice(q * columns, (q + 1) * columns)
            partial[rows, :] += jnp.dot(left, split[slot, q], preferred_element_type=jnp.float32)

    def body(step, carry):
        gather(step - 1)
        multiply(step)
        return carry

    def first_body(step, carry):
        fetch(step).wait()
        return body(step, carry)

    fetch(0).wait()
    multiply(jnp.int32(0))
    lax.fori_loop(1, middle, first_body, 0)
    for step in range(middle, steps):
        fetch(step).wait()
    nothing = jnp.zeros((size, size), jnp.bfloat16)

    def take(n):
        word = listed[n]
        field = lambda place, bits: lax.shift_right_logical(word, place) & ((1 << bits) - 1)
        b = field(8, 8)
        return turned[b], held[field(4, 4), b, field(0, 4)], field(16, 14)

    def project_ghosts(n, carry):
        for m in range(wide):
            left_a, block_a, target_a = take(n * 2 * wide + 2 * m)
            left_b, block_b, target_b = take(n * 2 * wide + 2 * m + 1)
            left = jnp.concatenate([left_a, left_b], axis=1)
            right = jnp.concatenate([
                jnp.concatenate([block_a, nothing], axis=1),
                jnp.concatenate([nothing, block_b], axis=1),
            ], axis=0)
            both = jnp.dot(left, right, preferred_element_type=jnp.float32)
            acc[target_a] += both[:, :size]
            acc[target_b] += both[:, size:]
        return carry

    lax.fori_loop(0, lax.div(found + 2 * wide - 1, 2 * wide), project_ghosts, 0)

    leaving = []
    for q in range(terms):
        for g in range(ghosts):
            staged[q, :, g * size:(g + 1) * size] = acc[q * ghosts + g].astype(jnp.bfloat16)
        leaving.append(pltpu.make_async_copy(staged.at[q], weights.at[q], went.at[q]))
        leaving[-1].start()
    lax.fori_loop(middle, steps, body, 0)
    gather(steps - 1)
    for copy in leaving:
        copy.wait()


def project(pattern, counts, exponents, values, matrices, parts, lent):
    kept, terms, owned = pattern.shape
    size = matrices.shape[-1]
    columns = values.shape[1]
    ghosts = parts + 2 * (lent - 1)
    weights = jax.ShapeDtypeStruct((terms, columns, ghosts * size), jnp.bfloat16)
    partial = jax.ShapeDtypeStruct((terms * columns, columns), jnp.float32)
    wide = 8
    return pl.pallas_call(
        functools.partial(project_kernel, parts, lent, owned // 3, wide),
        out_shape=(weights, partial),
        in_specs=[ANY] * 5,
        out_specs=(ANY, VMEM),
        scratch_shapes=[
            pltpu.VMEM((terms * ghosts + 1, columns, size), jnp.float32),
            pltpu.VMEM((owned + 1, size, columns), jnp.bfloat16),
            pltpu.VMEM((owned, columns, size), jnp.bfloat16),
            pltpu.VMEM((2, terms, 4 * size, columns), jnp.bfloat16),
            pltpu.VMEM(matrices.shape, jnp.bfloat16),
            pltpu.VMEM(weights.shape, weights.dtype),
            pltpu.VMEM(values.shape, values.dtype),
            pltpu.VMEM(pattern.shape, jnp.int32),
            pltpu.VMEM(counts.shape, jnp.int32),
            pltpu.VMEM(pattern.shape, jnp.int32),
            pltpu.VMEM(pattern.shape, jnp.int32),
            pltpu.SMEM(pattern.shape, jnp.int32),
            pltpu.SMEM(pattern.shape, jnp.int32),
            pltpu.SMEM(exponents.shape, jnp.int32),
            pltpu.SMEM((owned * terms * kept + 2 * wide,), jnp.int32),
            pltpu.SemaphoreType.DMA((owned // 2,)),
            pltpu.SemaphoreType.DMA((4,)),
            pltpu.SemaphoreType.DMA((2,)),
            pltpu.SemaphoreType.DMA((terms,)),
        ],
        compiler_params=pltpu.CompilerParams(vmem_limit_bytes=60 * 2**20),
        cost_estimate=pl.CostEstimate(
            flops=2 * matrices.size * columns, bytes_accessed=2 * matrices.size, transcendentals=0
        ),
        name="project",
    )(pattern, counts, exponents, values, matrices)


def finish_kernel(share, weights, far, below, above, own, keep, send):
    parity = lax.rem(lax.axis_index("dom"), 2)
    columns = own.shape[1]
    tile = max(columns, 2 * share)
    for first in range(0, own.shape[0], tile):
        rows = slice(first, first + tile)
        total = own[rows, :]
        start = 0
        for blocks in (far, below, above):
            stop = start + blocks.shape[0]
            total += jnp.dot(weights[rows, start:stop], blocks[...], preferred_element_type=jnp.float32)
            start = stop
        halves = total.reshape(-1, 2, share, columns)
        even = halves[:, 0].reshape(-1, columns)
        odd = halves[:, 1].reshape(-1, columns)
        half = slice(first // 2, (first + tile) // 2)
        keep[half, :] = jnp.where(parity == 0, even, odd)
        send[half, :] = jnp.where(parity == 0, odd, even)


def finish(weights, far, below, above, own, share):
    half = jax.ShapeDtypeStruct((own.shape[0] // 2, own.shape[1]), jnp.float32)
    return pl.pallas_call(
        functools.partial(finish_kernel, share),
        out_shape=(half, half),
        in_specs=[VMEM] * 5,
        out_specs=(VMEM, VMEM),
        compiler_params=pltpu.CompilerParams(vmem_limit_bytes=4 * 2**20),
        name="finish",
    )(weights, far, below, above, own)


def on_device(matrices, values, exponents, pattern, block_counts, send_lists, ghost_counts):
    parts = lax.axis_size("dom")
    terms = pattern.shape[0]
    size = matrices.shape[-1]
    lent = send_lists.shape[2]
    row_count, columns = values.shape

    far, after, before = pack(jnp.transpose(send_lists, (0, 2, 1)), exponents, values, size)
    far = lax.all_to_all(far, "dom", split_axis=0, concat_axis=0, tiled=True)
    below = lax.ppermute(after, "dom", [(p, p + 1) for p in range(parts - 1)])
    above = lax.ppermute(before, "dom", [(p + 1, p) for p in range(parts - 1)])

    weights, own = project(
        jnp.transpose(pattern, (2, 0, 1)), block_counts, exponents, values, matrices, parts, lent
    )
    share = terms * columns // parts
    flat = lambda a: a.reshape(-1, columns)
    keep, send = finish(weights.reshape(terms * columns, -1), flat(far), flat(below), flat(above), own, share)
    both = keep + lax.ppermute(send, "dom", [(p, p ^ 1) for p in range(parts)])
    both = both.astype(jnp.bfloat16).reshape(parts // 2, share, columns)
    groups = [list(range(core, parts, 2)) for core in range(2)]
    pieces = lax.all_to_all(both, "dom", split_axis=0, concat_axis=0, tiled=True, axis_index_groups=groups)
    summed = jnp.sum(pieces.astype(jnp.float32), axis=0)
    return summed * (1.0 / math.sqrt(row_count * parts))


def solution(mesh):
    return jax.shard_map(
        on_device,
        mesh=mesh,
        in_specs=(
            P(None, ("group", "dom"), None, None, None),
            P(("group", "dom"), None),
            P(("group", "dom")),
            P(None, ("group", "dom"), None),
            P(None, ("group", "dom")),
            P(("group", "dom"), None, None),
            P(("group", "dom"), None),
        ),
        out_specs=P(("group", "dom"), None),
        check_vma=False,
    )
```

time: 68.2 us -> 59.3 us (0.87); the launches traced: 67 us -> 58.9 us
  starting transfers between devices: 19.2 us -> 13.2 us
  local copies, waits for them, and re-layouts: 8.54 us -> 3.86 us
  Pallas kernels: 21.3 us -> 22.6 us
  waiting for transfers between devices: 1.54 us -> 2.67 us
    ppermute x1, starting transfers between devices: 8.25 us -> 2.22 us  [on_device(): both = keep + lax.ppermute(send, 'dom', [(p, p ^ 1) for p in range(parts)])]
    unnamed x12 -> x4, local copies, waits for them, and re-layouts: 8.54 us -> 3.86 us
    pallas_call x1, Pallas kernels: 16.9 us -> 18.2 us  [project(): pl.pallas_call(functools.partial(project_kernel, parts, lent, owned // 3,...]
    all_to_all x1, waiting for transfers between devices: 0.01 us -> 1.13 us  [on_device(): far = lax.all_to_all(far, 'dom', split_axis=0, concat_axis=0, tiled=True)]
  transfers between devices with their start and end apart: 4 -> 4, of which waited for: 1 -> 2; matrix products, arithmetic and copies ran while one was open for 0% -> 0% of each run, Pallas kernels for 25% -> 31%
where the time goes in v3:
time: 59.3 us; the launch traced here: 58.9 us
  Pallas kernels  22.6 us (38%)
  blocking collectives  15.7 us (26%)
  starting transfers between devices  13.2 us (22%)
  local copies, waits for them, and re-layouts  3.86 us (7%)
  waiting for transfers between devices  2.67 us (5%)
  other arithmetic  0.75 us (1%)
    pallas_call x1, Pallas kernels, project(): pl.pallas_call(functools.partial(project_kernel, parts, lent, owned // 3,...  18.2 us
    all_to_all x1, blocking collectives, on_device(): lax.all_to_all(both, 'dom', split_axis=0, concat_axis=0, tiled=True, axis...  15.7 us
    all_to_all x1, starting transfers between devices, on_device(): far = lax.all_to_all(far, 'dom', split_axis=0, concat_axis=0, tiled=True)  7.39 us
    unnamed x4, local copies, waits for them, and re-layouts  3.86 us
    pallas_call x1, Pallas kernels, pack(): pl.pallas_call(functools.partial(pack_kernel, parts, size), out_shape=(bl...  2.65 us
    ppermute x1, starting transfers between devices, on_device(): below = lax.ppermute(after, 'dom', [(p, p + 1) for p in range(parts - 1)])  2.31 us
    ppermute x1, starting transfers between devices, on_device(): both = keep + lax.ppermute(send, 'dom', [(p, p ^ 1) for p in range(parts)])  2.22 us
    pallas_call x1, Pallas kernels, finish(): pl.pallas_call(functools.partial(finish_kernel, share), out_shape=(half,...  1.79 us
  transfers between devices with their start and end apart: 4, of which 2 were waited for; matrix products, arithmetic and copies ran while one was open for 0% of the time, Pallas kernels for 31%

profile of v3, /device:TPU:0, one launch (start us, length us, event | category | flops | bytes accessed | tf_op | source)
XLA Modules:
  0.0 58.9 jit_solution(12305368771109237028)
XLA Ops:
  0.0 2.7 %pack.1 = (bf16[16,128,256]{2,1,0:T(8,128)(2,1)}, bf16[3,128,256]{2,1,0:T(8,128)(2,1)}, bf16[3,128,256]{2,1,0:T(8,128)(2,1)}) custom-call(s32[1,4,16]{2,1,0:T(4,128)} %bitcast.13, s32[24]{0:T(128)} %exponents.1, bf16[3072,256]{1,0:T(8,128)(2,1)} %values.1), custom_call_target="tpu_custom_call" | custom-call | tf_op jit(solution)/shard_map/pack/pallas_call | solution.py:41
  2.7 7.4 %all-to-all-start = ((bf16[16,128,256]{2,1,0:T(8,128)(2,1)}), bf16[16,128,256]{2,1,0:T(8,128)(2,1)S(1)}, u32[]{:S(2)}, u32[]{:S(2)}) async-start(bf16[16,128,256]{2,1,0:T(8,128)(2,1)} %get-tuple-element.13), calls=%async_computation | async-start | bytes 2097152 | tf_op jit(solution)/shard_map/all_to_all | solution.py:279
  10.0 2.3 %collective-permute-start = (bf16[3,128,256]{2,1,0:T(8,128)(2,1)}, bf16[3,128,256]{2,1,0:T(8,128)(2,1)S(1)}, u32[]{:S(2)}, u32[]{:S(2)}) collective-permute-start(bf16[3,128,256]{2,1,0:T(8,128)(2,1)} %get-tuple-element.14), channel_id=1, source_target_pairs={{0,1},{1,2},{2,3},{3,4},{4,5},{5,6},{6,7},{7,8},{8,9},{9,10},{10,1... | collective-permute-start | bytes 589832 | tf_op jit(solution)/shard_map/ppermute | solution.py:280
  12.4 1.3 %collective-permute-start.1 = (bf16[3,128,256]{2,1,0:T(8,128)(2,1)}, bf16[3,128,256]{2,1,0:T(8,128)(2,1)S(1)}, u32[]{:S(2)}, u32[]{:S(2)}) collective-permute-start(bf16[3,128,256]{2,1,0:T(8,128)(2,1)} %get-tuple-element.15), channel_id=1, source_target_pairs={{1,0},{2,1},{3,2},{4,3},{5,4},{6,5},{7,6},{8,7},{9,8},{10,9},{11,1... | collective-permute-start | bytes 589832 | tf_op jit(solution)/shard_map/ppermute | solution.py:281
  13.7 18.2 %project.1 = (bf16[4,256,2816]{2,1,0:T(8,128)(2,1)}, f32[1024,256]{1,0:T(8,128)}) custom-call(s32[6,4,24]{2,1,0:T(4,128)} %bitcast.12, s32[4,24]{1,0:T(4,128)} %counts_in.1, s32[24]{0:T(128)} %exponents.1, bf16[3072,256]{1,0:T(8,128)(2,1)} %values.1, bf16[4,24,6,128,128]{4,3,2,1,0:T(8,128)(2,1)} %matrices.1), custom_call_target="tpu_custom_call" | custom-call | flops 4831838208 | bytes 18874368 | tf_op jit(solution)/shard_map/project/pallas_call | solution.py:205
  31.8 0.0 collective-permute-done
  31.8 0.0 collective-permute-done.1
  31.9 1.1 %all-to-all-done = bf16[16,128,256]{2,1,0:T(8,128)(2,1)S(1)} async-done(((bf16[16,128,256]{2,1,0:T(8,128)(2,1)}), bf16[16,128,256]{2,1,0:T(8,128)(2,1)S(1)}, u32[]{:S(2)}, u32[]{:S(2)}) %all-to-all-start) | async-done | bytes 1048608 | tf_op jit(solution)/shard_map/all_to_all | solution.py:279
  33.0 0.0 copy-start
  33.0 2.6 %copy-done = bf16[4,256,2816]{2,1,0:T(8,128)(2,1)S(1)} copy-done((bf16[4,256,2816]{2,1,0:T(8,128)(2,1)S(1)}, bf16[4,256,2816]{2,1,0:T(8,128)(2,1)}, u32[]{:S(2)}) %copy-start) | copy-done | bytes 5767192
  35.6 0.0 copy-start.1
  35.6 1.2 %copy-done.1 = f32[1024,256]{1,0:T(8,128)S(1)} copy-done((f32[1024,256]{1,0:T(8,128)S(1)}, f32[1024,256]{1,0:T(8,128)}, u32[]{:S(2)}) %copy-start.1) | copy-done | bytes 1048600
  36.8 1.8 %finish.1 = (f32[512,256]{1,0:T(8,128)S(1)}, f32[512,256]{1,0:T(8,128)S(1)}) custom-call(bf16[1024,2816]{1,0:T(8,128)(2,1)S(1)} %bitcast.7, bf16[2048,256]{1,0:T(8,128)(2,1)S(1)} %bitcast.8, bf16[384,256]{1,0:T(8,128)(2,1)S(1)} %bitcast.9, bf16[384,256]{1,0:T(8,128)(2,1)S(1)} %bitcast.10, f32[1024,256]{1,0:T(8,128)S(1)} %copy-done.1), custom_call_target="tpu_custom_call" | custom-call | tf_op jit(solution)/shard_map/finish/pallas_call | solution.py:261
  38.6 2.2 %collective-permute-start.2 = (f32[512,256]{1,0:T(8,128)S(1)}, f32[512,256]{1,0:T(8,128)S(1)}, u32[]{:S(2)}, u32[]{:S(2)}) collective-permute-start(f32[512,256]{1,0:T(8,128)S(1)} %get-tuple-element.18), channel_id=1, source_target_pairs={{0,1},{1,0},{2,3},{3,2},{4,5},{5,4},{6,7},{7,6},{8,9},{9,8},{10,11... | collective-permute-start | bytes 1572872 | tf_op jit(solution)/shard_map/ppermute | solution.py:289
  40.9 1.5 %collective-permute-done.2 = f32[512,256]{1,0:T(8,128)S(1)} collective-permute-done((f32[512,256]{1,0:T(8,128)S(1)}, f32[512,256]{1,0:T(8,128)S(1)}, u32[]{:S(2)}, u32[]{:S(2)}) %collective-permute-start.2) | collective-permute-done | bytes 524320 | tf_op jit(solution)/shard_map/ppermute | solution.py:289
  42.4 0.1 add_convert_fusion
  42.5 15.7 %all_to_all.10 = bf16[8,64,256]{2,1,0:T(8,128)(2,1)S(1)} all-to-all(bf16[8,64,256]{2,1,0:T(8,128)(2,1)S(1)} %bitcast.11), channel_id=1, replica_groups={{0,2,4,6,8,10,12,14},{1,3,5,7,9,11,13,15},{16,18,20,22,24,26,28,30},{17..., dimensions={0} | all-to-all | bytes 524288 | tf_op jit(solution)/shard_map/all_to_all | solution.py:292
  58.2 0.6 %broadcast_multiply_fusion = f32[64,256]{1,0:T(8,128)} fusion(f32[64,256]{1,0:T(8,128)S(1)} %convert_reduce_fusion), kind=kLoop, calls=%fused_computation.2 | loop fusion | flops 16384 | bytes 131072 | tf_op jit(solution)/shard_map/mul | solution.py:294
  (1 shorter events, 0.0 us)
Async XLA Ops:
  2.7 30.3 %all-to-all-start = ((bf16[16,128,256]{2,1,0:T(8,128)(2,1)}), bf16[16,128,256]{2,1,0:T(8,128)(2,1)S(1)}, u32[]{:S(2)}, u32[]{:S(2)}) async-start(bf16[16,128,256]{2,1,0:T(8,128)(2,1)} %get-tuple-element.13), calls=%async_computation | async-start | bytes 2097152 | tf_op jit(solution)/shard_map/all_to_all | solution.py:279
  10.0 21.8 %collective-permute-start = (bf16[3,128,256]{2,1,0:T(8,128)(2,1)}, bf16[3,128,256]{2,1,0:T(8,128)(2,1)S(1)}, u32[]{:S(2)}, u32[]{:S(2)}) collective-permute-start(bf16[3,128,256]{2,1,0:T(8,128)(2,1)} %get-tuple-element.14), channel_id=1, source_target_pairs={{0,1},{1,2},{2,3},{3,4},{4,5},{5,6},{6,7},{7,8},{8,9},{9,10},{10,1... | collective-permute-start | bytes 589832 | tf_op jit(solution)/shard_map/ppermute | solution.py:280
  12.4 19.5 %collective-permute-start.1 = (bf16[3,128,256]{2,1,0:T(8,128)(2,1)}, bf16[3,128,256]{2,1,0:T(8,128)(2,1)S(1)}, u32[]{:S(2)}, u32[]{:S(2)}) collective-permute-start(bf16[3,128,256]{2,1,0:T(8,128)(2,1)} %get-tuple-element.15), channel_id=1, source_target_pairs={{1,0},{2,1},{3,2},{4,3},{5,4},{6,5},{7,6},{8,7},{9,8},{10,9},{11,1... | collective-permute-start | bytes 589832 | tf_op jit(solution)/shard_map/ppermute | solution.py:281
  33.0 2.6 %copy-start = (bf16[4,256,2816]{2,1,0:T(8,128)(2,1)S(1)}, bf16[4,256,2816]{2,1,0:T(8,128)(2,1)}, u32[]{:S(2)}) copy-start(bf16[4,256,2816]{2,1,0:T(8,128)(2,1)} %get-tuple-element.12) | copy-start | bytes 17301508
  35.6 1.2 %copy-start.1 = (f32[1024,256]{1,0:T(8,128)S(1)}, f32[1024,256]{1,0:T(8,128)}, u32[]{:S(2)}) copy-start(f32[1024,256]{1,0:T(8,128)} %get-tuple-element.16.own) | copy-start | bytes 3145732
  38.6 3.8 %collective-permute-start.2 = (f32[512,256]{1,0:T(8,128)S(1)}, f32[512,256]{1,0:T(8,128)S(1)}, u32[]{:S(2)}, u32[]{:S(2)}) collective-permute-start(f32[512,256]{1,0:T(8,128)S(1)} %get-tuple-element.18), channel_id=1, source_target_pairs={{0,1},{1,0},{2,3},{3,2},{4,5},{5,4},{6,7},{7,6},{8,9},{9,8},{10,11... | collective-permute-start | bytes 1572872 | tf_op jit(solution)/shard_map/ppermute | solution.py:289

commit v4 on v3

--- a/solution.py
+++ b/solution.py
@@ -47,11 +47,11 @@
     )(lists, exponents, values)
 
 
-def project_kernel(parts, lent, middle, wide, pattern_in, counts_in, exponents_in, values_in, matrices, *refs):
+def project_kernel(parts, lent, middle, wide, share, pattern_in, counts_in, exponents_in, values_in, matrices, *refs):
     kept, terms, owned = pattern_in.shape
-    weights, partial = refs[:2]
-    (acc, basis, turned, split, held, staged, values, pattern, counts, own_table, ghost_table,
-     own_slots, ghost_slots, exponents, listed, came, read, moved, went) = refs[2:]
+    outs = refs[:2]
+    (acc, basis, turned, split, held, staged, partial, values, pattern, counts,
+     own_table, ghost_table, own_slots, ghost_slots, exponents, listed, came, read, moved, went) = refs[2:]
     me = lax.axis_index("dom")
     size = held.shape[-1]
     columns = values.shape[1]
@@ -182,14 +182,39 @@
 
     lax.fori_loop(0, lax.div(found + 2 * wide - 1, 2 * wide), project_ghosts, 0)
 
+    parity = lax.rem(me, 2)
+    runs = columns // (2 * share)
+
+    def run(m, side):
+        return pl.ds(pl.multiple_of((2 * m + side) * share, share), share)
+
+    deep = ghosts * size
     leaving = []
-    for q in range(terms):
-        for g in range(ghosts):
-            staged[q, :, g * size:(g + 1) * size] = acc[q * ghosts + g].astype(jnp.bfloat16)
-        leaving.append(pltpu.make_async_copy(staged.at[q], weights.at[q], went.at[q]))
+
+    def leave(n, lanes):
+        leaving.append(pltpu.make_async_copy(staged.at[n, :, lanes], outs[n].at[:, lanes], went.at[len(leaving)]))
         leaving[-1].start()
+
+    sides = (1 - parity, parity)
+    for n, side in enumerate(sides):
+        for q in range(terms):
+            for m in range(runs):
+                rows = pl.ds((q * runs + m) * share, share)
+                for g in range(ghosts):
+                    lanes = slice(g * size, (g + 1) * size)
+                    staged[n, rows, lanes] = acc[q * ghosts + g, run(m, side), :].astype(jnp.bfloat16)
+        leave(n, slice(0, deep))
     lax.fori_loop(middle, steps, body, 0)
     gather(steps - 1)
+    for n, side in enumerate(sides):
+        for q in range(terms):
+            for m in range(runs):
+                exact = partial[pl.ds(pl.multiple_of(q * columns + (2 * m + side) * share, share), share), :]
+                upper = exact.astype(jnp.bfloat16)
+                rows = pl.ds((q * runs + m) * share, share)
+                staged[n, rows, deep:deep + columns] = upper
+                staged[n, rows, deep + columns:] = (exact - upper.astype(jnp.float32)).astype(jnp.bfloat16)
+        leave(n, slice(deep, deep + 2 * columns))
     for copy in leaving:
         copy.wait()
 
@@ -199,21 +224,21 @@
     size = matrices.shape[-1]
     columns = values.shape[1]
     ghosts = parts + 2 * (lent - 1)
-    weights = jax.ShapeDtypeStruct((terms, columns, ghosts * size), jnp.bfloat16)
-    partial = jax.ShapeDtypeStruct((terms * columns, columns), jnp.float32)
+    half = jax.ShapeDtypeStruct((terms * columns // 2, ghosts * size + 2 * columns), jnp.bfloat16)
     wide = 8
     return pl.pallas_call(
-        functools.partial(project_kernel, parts, lent, owned // 3, wide),
-        out_shape=(weights, partial),
+        functools.partial(project_kernel, parts, lent, owned // 3, wide, terms * columns // parts),
+        out_shape=(half, half),
         in_specs=[ANY] * 5,
-        out_specs=(ANY, VMEM),
+        out_specs=(ANY, ANY),
         scratch_shapes=[
             pltpu.VMEM((terms * ghosts + 1, columns, size), jnp.float32),
             pltpu.VMEM((owned + 1, size, columns), jnp.bfloat16),
             pltpu.VMEM((owned, columns, size), jnp.bfloat16),
             pltpu.VMEM((2, terms, 4 * size, columns), jnp.bfloat16),
             pltpu.VMEM(matrices.shape, jnp.bfloat16),
-            pltpu.VMEM(weights.shape, weights.dtype),
+            pltpu.VMEM((2,) + half.shape, half.dtype),
+            pltpu.VMEM((terms * columns, columns), jnp.float32),
             pltpu.VMEM(values.shape, values.dtype),
             pltpu.VMEM(pattern.shape, jnp.int32),
             pltpu.VMEM(counts.shape, jnp.int32),
@@ -226,7 +251,7 @@
             pltpu.SemaphoreType.DMA((owned // 2,)),
             pltpu.SemaphoreType.DMA((4,)),
             pltpu.SemaphoreType.DMA((2,)),
-            pltpu.SemaphoreType.DMA((terms,)),
+            pltpu.SemaphoreType.DMA((4,)),
         ],
         compiler_params=pltpu.CompilerParams(vmem_limit_bytes=60 * 2**20),
         cost_estimate=pl.CostEstimate(
@@ -236,36 +261,31 @@
     )(pattern, counts, exponents, values, matrices)
 
 
-def finish_kernel(share, weights, far, below, above, own, keep, send):
-    parity = lax.rem(lax.axis_index("dom"), 2)
-    columns = own.shape[1]
-    tile = max(columns, 2 * share)
-    for first in range(0, own.shape[0], tile):
-        rows = slice(first, first + tile)
-        total = own[rows, :]
-        start = 0
-        for blocks in (far, below, above):
-            stop = start + blocks.shape[0]
-            total += jnp.dot(weights[rows, start:stop], blocks[...], preferred_element_type=jnp.float32)
-            start = stop
-        halves = total.reshape(-1, 2, share, columns)
-        even = halves[:, 0].reshape(-1, columns)
-        odd = halves[:, 1].reshape(-1, columns)
-        half = slice(first // 2, (first + tile) // 2)
-        keep[half, :] = jnp.where(parity == 0, even, odd)
-        send[half, :] = jnp.where(parity == 0, odd, even)
-
-
-def finish(weights, far, below, above, own, share):
-    half = jax.ShapeDtypeStruct((own.shape[0] // 2, own.shape[1]), jnp.float32)
+def half_kernel(weights, far, below, above, out):
+    columns = out.shape[1]
+    deep = weights.shape[1] - 2 * columns
+    total = weights[:, deep:deep + columns].astype(jnp.float32) + weights[:, deep + columns:].astype(jnp.float32)
+    start = 0
+    for block in (far, below, above):
+        stop = start + block.shape[0]
+        total += jnp.dot(weights[:, start:stop], block[...], preferred_element_type=jnp.float32)
+        start = stop
+    out[...] = total
+
+
+def half_partial(weights, far, below, above):
+    rows, columns = weights.shape[0], far.shape[1]
     return pl.pallas_call(
-        functools.partial(finish_kernel, share),
-        out_shape=(half, half),
-        in_specs=[VMEM] * 5,
-        out_specs=(VMEM, VMEM),
+        half_kernel,
+        out_shape=jax.ShapeDtypeStruct((rows, columns), jnp.float32),
+        in_specs=[VMEM] * 4,
+        out_specs=VMEM,
         compiler_params=pltpu.CompilerParams(vmem_limit_bytes=4 * 2**20),
-        name="finish",
-    )(weights, far, below, above, own)
+        cost_estimate=pl.CostEstimate(
+            flops=2 * weights.size * columns, bytes_accessed=2 * weights.size, transcendentals=0
+        ),
+        name="half_partial",
+    )(weights, far, below, above)
 
 
 def on_device(matrices, values, exponents, pattern, block_counts, send_lists, ghost_counts):
@@ -280,13 +300,15 @@
     below = lax.ppermute(after, "dom", [(p, p + 1) for p in range(parts - 1)])
     above = lax.ppermute(before, "dom", [(p + 1, p) for p in range(parts - 1)])
 
-    weights, own = project(
+    send_weights, keep_weights = project(
         jnp.transpose(pattern, (2, 0, 1)), block_counts, exponents, values, matrices, parts, lent
     )
+    flat = lambda a: a.reshape(-1, columns)
+    ghosts = (flat(far), flat(below), flat(above))
+    send = half_partial(send_weights, *ghosts)
+    came = lax.ppermute(send, "dom", [(p, p ^ 1) for p in range(parts)])
+    both = came + half_partial(keep_weights, *ghosts)
     share = terms * columns // parts
-    flat = lambda a: a.reshape(-1, columns)
-    keep, send = finish(weights.reshape(terms * columns, -1), flat(far), flat(below), flat(above), own, share)
-    both = keep + lax.ppermute(send, "dom", [(p, p ^ 1) for p in range(parts)])
     both = both.astype(jnp.bfloat16).reshape(parts // 2, share, columns)
     groups = [list(range(core, parts, 2)) for core in range(2)]
     pieces = lax.all_to_all(both, "dom", split_axis=0, concat_axis=0, tiled=True, axis_index_groups=groups)

time: 59.3 us -> 57.1 us (0.963)
  local copies, waits for them, and re-layouts: 3.86 us -> 2.12 us
  waiting for transfers between devices: 2.67 us -> 1.48 us
    unnamed x4, local copies, waits for them, and re-layouts: 3.86 us -> 2.12 us
    ppermute x1, waiting for transfers between devices: 1.54 us -> 0.55 us  [on_device(): came = lax.ppermute(send, 'dom', [(p, p ^ 1) for p in range(parts)])]
    pallas_call x1 -> x2, Pallas kernels: 1.79 us -> 1.95 us  [half_partial(): pl.pallas_call(half_kernel, out_shape=jax.ShapeDtypeStruct((rows, columns...]
  transfers between devices with their start and end apart: 4 -> 4, of which waited for: 2 -> 2; matrix products, arithmetic and copies ran while one was open for 0% -> 0% of each run, Pallas kernels for 31% -> 34%
where the time goes in v4:
time: 57.1 us; the launch traced here: 56.3 us
  Pallas kernels  23 us (40%)
  blocking collectives  15.5 us (27%)
  starting transfers between devices  13.4 us (23%)
  local copies, waits for them, and re-layouts  2.12 us (4%)
  waiting for transfers between devices  1.48 us (3%)
  other arithmetic  0.75 us (1%)
    pallas_call x1, Pallas kernels, project(): pl.pallas_call(functools.partial(project_kernel, parts, lent, owned // 3,...  18.4 us
    all_to_all x1, blocking collectives, on_device(): lax.all_to_all(both, 'dom', split_axis=0, concat_axis=0, tiled=True, axis...  15.5 us
    all_to_all x1, starting transfers between devices, on_device(): far = lax.all_to_all(far, 'dom', split_axis=0, concat_axis=0, tiled=True)  7.39 us
    pallas_call x1, Pallas kernels, pack(): pl.pallas_call(functools.partial(pack_kernel, parts, size), out_shape=(bl...  2.66 us
    ppermute x1, starting transfers between devices, on_device(): came = lax.ppermute(send, 'dom', [(p, p ^ 1) for p in range(parts)])  2.42 us
    ppermute x1, starting transfers between devices, on_device(): below = lax.ppermute(after, 'dom', [(p, p + 1) for p in range(parts - 1)])  2.31 us
    unnamed x4, local copies, waits for them, and re-layouts  2.12 us
    pallas_call x2, Pallas kernels, half_partial(): pl.pallas_call(half_kernel, out_shape=jax.ShapeDtypeStruct((rows, columns...  1.95 us
  transfers between devices with their start and end apart: 4, of which 2 were waited for; matrix products, arithmetic and copies ran while one was open for 0% of the time, Pallas kernels for 34%

profile of v4, /device:TPU:0, one launch (start us, length us, event | category | flops | bytes accessed | tf_op | source)
XLA Modules:
  0.0 56.3 jit_solution(10856868358025752751)
XLA Ops:
  0.0 2.7 %pack.1 = (bf16[16,128,256]{2,1,0:T(8,128)(2,1)}, bf16[3,128,256]{2,1,0:T(8,128)(2,1)}, bf16[3,128,256]{2,1,0:T(8,128)(2,1)}) custom-call(s32[1,4,16]{2,1,0:T(4,128)} %bitcast.14, s32[24]{0:T(128)} %exponents.1, bf16[3072,256]{1,0:T(8,128)(2,1)} %values.1), custom_call_target="tpu_custom_call" | custom-call | tf_op jit(solution)/shard_map/pack/pallas_call | solution.py:41
  2.7 7.4 %all-to-all-start = ((bf16[16,128,256]{2,1,0:T(8,128)(2,1)}), bf16[16,128,256]{2,1,0:T(8,128)(2,1)S(1)}, u32[]{:S(2)}, u32[]{:S(2)}) async-start(bf16[16,128,256]{2,1,0:T(8,128)(2,1)} %get-tuple-element.11), calls=%async_computation | async-start | bytes 2097152 | tf_op jit(solution)/shard_map/all_to_all | solution.py:299
  10.1 2.3 %collective-permute-start = (bf16[3,128,256]{2,1,0:T(8,128)(2,1)}, bf16[3,128,256]{2,1,0:T(8,128)(2,1)S(1)}, u32[]{:S(2)}, u32[]{:S(2)}) collective-permute-start(bf16[3,128,256]{2,1,0:T(8,128)(2,1)} %get-tuple-element.12), channel_id=1, source_target_pairs={{0,1},{1,2},{2,3},{3,4},{4,5},{5,6},{6,7},{7,8},{8,9},{9,10},{10,1... | collective-permute-start | bytes 589832 | tf_op jit(solution)/shard_map/ppermute | solution.py:300
  12.4 1.3 %collective-permute-start.1 = (bf16[3,128,256]{2,1,0:T(8,128)(2,1)}, bf16[3,128,256]{2,1,0:T(8,128)(2,1)S(1)}, u32[]{:S(2)}, u32[]{:S(2)}) collective-permute-start(bf16[3,128,256]{2,1,0:T(8,128)(2,1)} %get-tuple-element.13), channel_id=1, source_target_pairs={{1,0},{2,1},{3,2},{4,3},{5,4},{6,5},{7,6},{8,7},{9,8},{10,9},{11,1... | collective-permute-start | bytes 589832 | tf_op jit(solution)/shard_map/ppermute | solution.py:301
  13.7 18.4 %project.1 = (bf16[512,3328]{1,0:T(8,128)(2,1)}, bf16[512,3328]{1,0:T(8,128)(2,1)}) custom-call(s32[6,4,24]{2,1,0:T(4,128)} %bitcast.13, s32[4,24]{1,0:T(4,128)} %counts_in.1, s32[24]{0:T(128)} %exponents.1, bf16[3072,256]{1,0:T(8,128)(2,1)} %values.1, bf16[4,24,6,128,128]{4,3,2,1,0:T(8,128)(2,1)} %matrices.1), custom_call_target="tpu_custom_call" | custom-call | flops 4831838208 | bytes 18874368 | tf_op jit(solution)/shard_map/project/pallas_call | solution.py:229
  32.0 0.0 collective-permute-done
  32.1 0.0 collective-permute-done.1
  32.1 0.9 %all-to-all-done = bf16[16,128,256]{2,1,0:T(8,128)(2,1)S(1)} async-done(((bf16[16,128,256]{2,1,0:T(8,128)(2,1)}), bf16[16,128,256]{2,1,0:T(8,128)(2,1)S(1)}, u32[]{:S(2)}, u32[]{:S(2)}) %all-to-all-start) | async-done | bytes 1048608 | tf_op jit(solution)/shard_map/all_to_all | solution.py:299
  33.0 0.0 copy-start
  33.0 0.0 copy-start.1
  33.0 2.1 %copy-done.1 = bf16[512,3328]{1,0:T(8,128)(2,1)S(1)} copy-done((bf16[512,3328]{1,0:T(8,128)(2,1)S(1)}, bf16[512,3328]{1,0:T(8,128)(2,1)}, u32[]{:S(2)}) %copy-start.1) | copy-done | bytes 3407896
  35.1 1.0 %half_partial.2 = f32[512,256]{1,0:T(8,128)S(1)} custom-call(bf16[512,3328]{1,0:T(8,128)(2,1)S(1)} %copy-done.1, bf16[2048,256]{1,0:T(8,128)(2,1)S(1)} %bitcast.6, bf16[384,256]{1,0:T(8,128)(2,1)S(1)} %bitcast.8, bf16[384,256]{1,0:T(8,128)(2,1)S(1)} %bitcast.10), custom_call_target="tpu_custom_call" | custom-call | flops 872415232 | bytes 3407872 | tf_op jit(solution)/shard_map/half_partial/pallas_call | solution.py:278
  36.1 2.4 %collective-permute-start.2 = (f32[512,256]{1,0:T(8,128)S(1)}, f32[512,256]{1,0:T(8,128)S(1)}, u32[]{:S(2)}, u32[]{:S(2)}) collective-permute-start(f32[512,256]{1,0:T(8,128)S(1)} %half_partial.2), channel_id=1, source_target_pairs={{0,1},{1,0},{2,3},{3,2},{4,5},{5,4},{6,7},{7,6},{8,9},{9,8},{10,11... | collective-permute-start | bytes 1572872 | tf_op jit(solution)/shard_map/ppermute | solution.py:309
  38.5 0.0 copy-done
  38.5 1.0 %half_partial.3 = f32[512,256]{1,0:T(8,128)S(1)} custom-call(bf16[512,3328]{1,0:T(8,128)(2,1)S(1)} %copy-done, bf16[2048,256]{1,0:T(8,128)(2,1)S(1)} %bitcast.7, bf16[384,256]{1,0:T(8,128)(2,1)S(1)} %bitcast.9, bf16[384,256]{1,0:T(8,128)(2,1)S(1)} %bitcast.11), custom_call_target="tpu_custom_call" | custom-call | flops 872415232 | bytes 3407872 | tf_op jit(solution)/shard_map/half_partial/pallas_call | solution.py:278
  39.5 0.6 collective-permute-done.2
  40.1 0.1 add_convert_fusion
  40.1 15.5 %all_to_all.10 = bf16[8,64,256]{2,1,0:T(8,128)(2,1)S(1)} all-to-all(bf16[8,64,256]{2,1,0:T(8,128)(2,1)S(1)} %bitcast.12), channel_id=1, replica_groups={{0,2,4,6,8,10,12,14},{1,3,5,7,9,11,13,15},{16,18,20,22,24,26,28,30},{17..., dimensions={0} | all-to-all | bytes 524288 | tf_op jit(solution)/shard_map/all_to_all | solution.py:314
  55.7 0.6 %broadcast_multiply_fusion = f32[64,256]{1,0:T(8,128)} fusion(f32[64,256]{1,0:T(8,128)S(1)} %convert_reduce_fusion), kind=kLoop, calls=%fused_computation.2 | loop fusion | flops 16384 | bytes 131072 | tf_op jit(solution)/shard_map/mul | solution.py:316
  (1 shorter events, 0.0 us)
Async XLA Ops:
  2.7 30.3 %all-to-all-start = ((bf16[16,128,256]{2,1,0:T(8,128)(2,1)}), bf16[16,128,256]{2,1,0:T(8,128)(2,1)S(1)}, u32[]{:S(2)}, u32[]{:S(2)}) async-start(bf16[16,128,256]{2,1,0:T(8,128)(2,1)} %get-tuple-element.11), calls=%async_computation | async-start | bytes 2097152 | tf_op jit(solution)/shard_map/all_to_all | solution.py:299
  10.1 22.0 %collective-permute-start = (bf16[3,128,256]{2,1,0:T(8,128)(2,1)}, bf16[3,128,256]{2,1,0:T(8,128)(2,1)S(1)}, u32[]{:S(2)}, u32[]{:S(2)}) collective-permute-start(bf16[3,128,256]{2,1,0:T(8,128)(2,1)} %get-tuple-element.12), channel_id=1, source_target_pairs={{0,1},{1,2},{2,3},{3,4},{4,5},{5,6},{6,7},{7,8},{8,9},{9,10},{10,1... | collective-permute-start | bytes 589832 | tf_op jit(solution)/shard_map/ppermute | solution.py:300
  12.4 19.7 %collective-permute-start.1 = (bf16[3,128,256]{2,1,0:T(8,128)(2,1)}, bf16[3,128,256]{2,1,0:T(8,128)(2,1)S(1)}, u32[]{:S(2)}, u32[]{:S(2)}) collective-permute-start(bf16[3,128,256]{2,1,0:T(8,128)(2,1)} %get-tuple-element.13), channel_id=1, source_target_pairs={{1,0},{2,1},{3,2},{4,3},{5,4},{6,5},{7,6},{8,7},{9,8},{10,9},{11,1... | collective-permute-start | bytes 589832 | tf_op jit(solution)/shard_map/ppermute | solution.py:301
  33.0 5.5 %copy-start = (bf16[512,3328]{1,0:T(8,128)(2,1)S(1)}, bf16[512,3328]{1,0:T(8,128)(2,1)}, u32[]{:S(2)}) copy-start(bf16[512,3328]{1,0:T(8,128)(2,1)} %get-tuple-element.14.weights) | copy-start | bytes 10223620
  33.0 2.1 %copy-start.1 = (bf16[512,3328]{1,0:T(8,128)(2,1)S(1)}, bf16[512,3328]{1,0:T(8,128)(2,1)}, u32[]{:S(2)}) copy-start(bf16[512,3328]{1,0:T(8,128)(2,1)} %get-tuple-element.10.weights) | copy-start | bytes 10223620
  36.1 4.0 %collective-permute-start.2 = (f32[512,256]{1,0:T(8,128)S(1)}, f32[512,256]{1,0:T(8,128)S(1)}, u32[]{:S(2)}, u32[]{:S(2)}) collective-permute-start(f32[512,256]{1,0:T(8,128)S(1)} %half_partial.2), channel_id=1, source_target_pairs={{0,1},{1,0},{2,3},{3,2},{4,5},{5,4},{6,7},{7,6},{8,9},{9,8},{10,11... | collective-permute-start | bytes 1572872 | tf_op jit(solution)/shard_map/ppermute | solution.py:309

commit v5 on v4

--- a/solution.py
+++ b/solution.py
@@ -17,11 +17,15 @@
     return (lax.shift_left(jnp.int32(1), exponent + 2).astype(jnp.float32) * 0.25).astype(jnp.bfloat16)
 
 
-def pack_kernel(parts, size, lists, exponents, values, far, after, before):
+def neighbours(me, parts):
+    parity = lax.rem(me, 2)
+    return me + 1 - 2 * parity, jnp.clip(me - 1 + 2 * parity, 0, parts - 1)
+
+
+def pack_kernel(parts, size, lists, exponents, values, far, inner, outer):
     me = lax.axis_index("dom")
     lent = lists.shape[1]
-    upper = jnp.minimum(me + 1, parts - 1)
-    lower = jnp.maximum(me - 1, 0)
+    mate, other = neighbours(me, parts)
 
     def lend(block, out, n):
         rows = pl.ds(pl.multiple_of(block * size, size), size)
@@ -30,8 +34,8 @@
     for p in range(parts):
         lend(lists[0, 0, p], far, p)
     for g in range(1, lent):
-        lend(lists[0, g, upper], after, g - 1)
-        lend(lists[0, g, lower], before, g - 1)
+        lend(lists[0, g, mate], inner, g - 1)
+        lend(lists[0, g, other], outer, g - 1)
 
 
 def pack(lists, exponents, values, size):
@@ -55,6 +59,7 @@
     me = lax.axis_index("dom")
     size = held.shape[-1]
     columns = values.shape[1]
+    mate, _ = neighbours(me, parts)
     ghosts = parts + 2 * (lent - 1)
     trash = terms * ghosts
     steps = owned // 2
@@ -89,7 +94,7 @@
     present = k < counts[...][None]
     ghost = present & (slot >= owned)
     lender, which = (slot - owned) // lent, (slot - owned) % lent
-    further = parts + which - 1 + jnp.where(lender > me, lent - 1, 0)
+    further = parts + which - 1 + jnp.where(lender == mate, 0, lent - 1)
     target = q * ghosts + jnp.where(which == 0, lender, further)
     some = jnp.max(ghost.astype(jnp.int32), axis=0, keepdims=True)
     own_table[...] = jnp.where(present & (slot < owned), slot, owned) + jnp.where(k == 0, 256 * some, 0)
@@ -261,31 +266,40 @@
     )(pattern, counts, exponents, values, matrices)
 
 
-def half_kernel(weights, far, below, above, out):
+def far_kernel(weights, far, out):
     columns = out.shape[1]
     deep = weights.shape[1] - 2 * columns
     total = weights[:, deep:deep + columns].astype(jnp.float32) + weights[:, deep + columns:].astype(jnp.float32)
-    start = 0
-    for block in (far, below, above):
-        stop = start + block.shape[0]
-        total += jnp.dot(weights[:, start:stop], block[...], preferred_element_type=jnp.float32)
-        start = stop
-    out[...] = total
-
-
-def half_partial(weights, far, below, above):
-    rows, columns = weights.shape[0], far.shape[1]
+    out[...] = total + jnp.dot(weights[:, :far.shape[0]], far[...], preferred_element_type=jnp.float32)
+
+
+def near_kernel(weights, total, far, inner, outer, out):
+    start = far.shape[0]
+    middle = start + inner.shape[0]
+    stop = middle + outer.shape[0]
+    near = jnp.dot(weights[:, start:middle], inner[...], preferred_element_type=jnp.float32)
+    near += jnp.dot(weights[:, middle:stop], outer[...], preferred_element_type=jnp.float32)
+    out[...] = total[...] + near
+
+
+def half_kernel(weights, far, inner, outer, out):
+    far_kernel(weights, far, out)
+    near_kernel(weights, out, far, inner, outer, out)
+
+
+def half_partial(kernel, weights, *blocks):
+    rows, columns = weights.shape[0], blocks[-1].shape[1]
     return pl.pallas_call(
-        half_kernel,
+        kernel,
         out_shape=jax.ShapeDtypeStruct((rows, columns), jnp.float32),
-        in_specs=[VMEM] * 4,
+        in_specs=[VMEM] * (1 + len(blocks)),
         out_specs=VMEM,
         compiler_params=pltpu.CompilerParams(vmem_limit_bytes=4 * 2**20),
         cost_estimate=pl.CostEstimate(
             flops=2 * weights.size * columns, bytes_accessed=2 * weights.size, transcendentals=0
         ),
-        name="half_partial",
-    )(weights, far, below, above)
+        name=kernel.__name__,
+    )(weights, *blocks)
 
 
 def on_device(matrices, values, exponents, pattern, block_counts, send_lists, ghost_counts):
@@ -295,19 +309,22 @@
     lent = send_lists.shape[2]
     row_count, columns = values.shape
 
-    far, after, before = pack(jnp.transpose(send_lists, (0, 2, 1)), exponents, values, size)
+    far, inner, outer = pack(jnp.transpose(send_lists, (0, 2, 1)), exponents, values, size)
+    mates = [(p, p ^ 1) for p in range(parts)]
+    others = [(p, q) for n in range(1, parts - 1, 2) for p, q in ((n, n + 1), (n + 1, n))]
     far = lax.all_to_all(far, "dom", split_axis=0, concat_axis=0, tiled=True)
-    below = lax.ppermute(after, "dom", [(p, p + 1) for p in range(parts - 1)])
-    above = lax.ppermute(before, "dom", [(p + 1, p) for p in range(parts - 1)])
+    outer = lax.ppermute(outer, "dom", others)
+    inner = lax.ppermute(inner, "dom", mates)
 
     send_weights, keep_weights = project(
         jnp.transpose(pattern, (2, 0, 1)), block_counts, exponents, values, matrices, parts, lent
     )
     flat = lambda a: a.reshape(-1, columns)
-    ghosts = (flat(far), flat(below), flat(above))
-    send = half_partial(send_weights, *ghosts)
-    came = lax.ppermute(send, "dom", [(p, p ^ 1) for p in range(parts)])
-    both = came + half_partial(keep_weights, *ghosts)
+    far, inner, outer = flat(far), flat(inner), flat(outer)
+    send = half_partial(far_kernel, send_weights, far)
+    send = half_partial(near_kernel, send_weights, send, far, inner, outer)
+    came = lax.ppermute(send, "dom", mates)
+    both = came + half_partial(half_kernel, keep_weights, far, inner, outer)
     share = terms * columns // parts
     both = both.astype(jnp.bfloat16).reshape(parts // 2, share, columns)
     groups = [list(range(core, parts, 2)) for core in range(2)]

time: 57.1 us -> 55.7 us (0.975)
  starting transfers between devices: 13.4 us -> 9.13 us
  waiting for transfers between devices: 1.48 us -> 4.02 us
  local copies, waits for them, and re-layouts: 2.12 us -> 2.8 us
    ppermute x3, starting transfers between devices: 6.03 us -> 1.74 us  [the longest x1 0.67 us: on_device(): came = lax.ppermute(send, 'dom', mates)]
    all_to_all x1, waiting for transfers between devices: 0.93 us -> 4.02 us  [on_device(): far = lax.all_to_all(far, 'dom', split_axis=0, concat_axis=0, tiled=True)]
    unnamed x4, local copies, waits for them, and re-layouts: 2.12 us -> 2.8 us
    pallas_call x2 -> x3, Pallas kernels: 1.95 us -> 2.1 us  [half_partial(): pl.pallas_call(kernel, out_shape=jax.ShapeDtypeStruct((rows, columns), jn...]
  transfers between devices with their start and end apart: 4 -> 4, of which waited for: 2 -> 1; matrix products, arithmetic and copies ran while one was open for 0% -> 0% of each run, Pallas kernels for 34% -> 35%
where the time goes in v5:
time: 55.7 us; the launch traced here: 55.4 us
  Pallas kernels  22.6 us (41%)
  blocking collectives  16 us (29%)
  starting transfers between devices  9.13 us (16%)
  waiting for transfers between devices  4.02 us (7%)
  local copies, waits for them, and re-layouts  2.8 us (5%)
  other arithmetic  0.75 us (1%)
    pallas_call x1, Pallas kernels, project(): pl.pallas_call(functools.partial(project_kernel, parts, lent, owned // 3,...  17.8 us
    all_to_all x1, blocking collectives, on_device(): lax.all_to_all(both, 'dom', split_axis=0, concat_axis=0, tiled=True, axis...  16 us
    all_to_all x1, starting transfers between devices, on_device(): far = lax.all_to_all(far, 'dom', split_axis=0, concat_axis=0, tiled=True)  7.39 us
    all_to_all x1, waiting for transfers between devices, on_device(): far = lax.all_to_all(far, 'dom', split_axis=0, concat_axis=0, tiled=True)  4.02 us
    unnamed x4, local copies, waits for them, and re-layouts  2.8 us
    pallas_call x1, Pallas kernels, pack(): pl.pallas_call(functools.partial(pack_kernel, parts, size), out_shape=(bl...  2.64 us
    pallas_call x3, Pallas kernels, half_partial(): pl.pallas_call(kernel, out_shape=jax.ShapeDtypeStruct((rows, columns), jn...  2.1 us
  transfers between devices with their start and end apart: 4, of which 1 were waited for; matrix products, arithmetic and copies ran while one was open for 0% of the time, Pallas kernels for 35%

profile of v5, /device:TPU:0, one launch (start us, length us, event | category | flops | bytes accessed | tf_op | source)
XLA Modules:
  0.0 55.4 jit_solution(17627929270692702708)
XLA Ops:
  0.0 2.6 %pack.1 = (bf16[16,128,256]{2,1,0:T(8,128)(2,1)}, bf16[3,128,256]{2,1,0:T(8,128)(2,1)}, bf16[3,128,256]{2,1,0:T(8,128)(2,1)}) custom-call(s32[1,4,16]{2,1,0:T(4,128)} %bitcast.15, s32[24]{0:T(128)} %exponents.1, bf16[3072,256]{1,0:T(8,128)(2,1)} %values.1), custom_call_target="tpu_custom_call" | custom-call | tf_op jit(solution)/shard_map/pack/pallas_call | solution.py:45
  2.6 7.4 %all-to-all-start = ((bf16[16,128,256]{2,1,0:T(8,128)(2,1)}), bf16[16,128,256]{2,1,0:T(8,128)(2,1)S(1)}, u32[]{:S(2)}, u32[]{:S(2)}) async-start(bf16[16,128,256]{2,1,0:T(8,128)(2,1)} %get-tuple-element.11), calls=%async_computation | async-start | bytes 2097152 | tf_op jit(solution)/shard_map/all_to_all | solution.py:315
  10.0 0.4 collective-permute-start
  10.4 0.7 %collective-permute-start.1 = (bf16[3,128,256]{2,1,0:T(8,128)(2,1)}, bf16[3,128,256]{2,1,0:T(8,128)(2,1)S(1)}, u32[]{:S(2)}, u32[]{:S(2)}) collective-permute-start(bf16[3,128,256]{2,1,0:T(8,128)(2,1)} %get-tuple-element.13), channel_id=1, source_target_pairs={{1,2},{2,1},{3,4},{4,3},{5,6},{6,5},{7,8},{8,7},{9,10},{10,9},{11,... | collective-permute-start | bytes 589832 | tf_op jit(solution)/shard_map/ppermute | solution.py:316
  11.1 17.8 %project.1 = (bf16[512,3328]{1,0:T(8,128)(2,1)}, bf16[512,3328]{1,0:T(8,128)(2,1)}) custom-call(s32[6,4,24]{2,1,0:T(4,128)} %bitcast.14, s32[4,24]{1,0:T(4,128)} %counts_in.1, s32[24]{0:T(128)} %exponents.1, bf16[3072,256]{1,0:T(8,128)(2,1)} %values.1, bf16[4,24,6,128,128]{4,3,2,1,0:T(8,128)(2,1)} %matrices.1), custom_call_target="tpu_custom_call" | custom-call | flops 4831838208 | bytes 18874368 | tf_op jit(solution)/shard_map/project/pallas_call | solution.py:234
  29.0 4.0 %all-to-all-done = bf16[16,128,256]{2,1,0:T(8,128)(2,1)S(1)} async-done(((bf16[16,128,256]{2,1,0:T(8,128)(2,1)}), bf16[16,128,256]{2,1,0:T(8,128)(2,1)S(1)}, u32[]{:S(2)}, u32[]{:S(2)}) %all-to-all-start) | async-done | bytes 1048608 | tf_op jit(solution)/shard_map/all_to_all | solution.py:315
  33.0 0.0 copy-start
  33.0 2.0 %copy-done = bf16[512,3328]{1,0:T(8,128)(2,1)S(1)} copy-done((bf16[512,3328]{1,0:T(8,128)(2,1)S(1)}, bf16[512,3328]{1,0:T(8,128)(2,1)}, u32[]{:S(2)}) %copy-start) | copy-done | bytes 3407896
  34.9 0.7 %far_kernel.1.total = f32[512,256]{1,0:T(8,128)S(1)} custom-call(bf16[512,3328]{1,0:T(8,128)(2,1)S(1)} %copy-done, bf16[2048,256]{1,0:T(8,128)(2,1)S(1)} %bitcast.6), custom_call_target="tpu_custom_call" | custom-call | flops 872415232 | bytes 3407872 | tf_op jit(solution)/shard_map/far_kernel/pallas_call | solution.py:292
  35.7 0.0 copy-start.1
  35.7 0.0 collective-permute-done
  35.7 0.0 collective-permute-done.1
  35.7 0.4 near_kernel.1
  36.1 0.7 %collective-permute-start.2 = (f32[512,256]{1,0:T(8,128)S(1)}, f32[512,256]{1,0:T(8,128)S(1)}, u32[]{:S(2)}, u32[]{:S(2)}) collective-permute-start(f32[512,256]{1,0:T(8,128)S(1)} %near_kernel.1), channel_id=1, source_target_pairs={{0,1},{1,0},{2,3},{3,2},{4,5},{5,4},{6,7},{7,6},{8,9},{9,8},{10,11... | collective-permute-start | bytes 1572872 | tf_op jit(solution)/shard_map/ppermute | solution.py:326
  36.8 0.8 %copy-done.1 = bf16[512,3328]{1,0:T(8,128)(2,1)S(1)} copy-done((bf16[512,3328]{1,0:T(8,128)(2,1)S(1)}, bf16[512,3328]{1,0:T(8,128)(2,1)}, u32[]{:S(2)}) %copy-start.1) | copy-done | bytes 3407896
  37.6 1.0 %half_kernel.1 = f32[512,256]{1,0:T(8,128)S(1)} custom-call(bf16[512,3328]{1,0:T(8,128)(2,1)S(1)} %copy-done.1, bf16[2048,256]{1,0:T(8,128)(2,1)S(1)} %bitcast.8, bf16[384,256]{1,0:T(8,128)(2,1)S(1)} %bitcast.10, bf16[384,256]{1,0:T(8,128)(2,1)S(1)} %bitcast.12), custom_call_target="tpu_custom_call" | custom-call | flops 872415232 | bytes 3407872 | tf_op jit(solution)/shard_map/half_kernel/pallas_call | solution.py:292
  38.6 0.0 collective-permute-done.2
  38.6 0.1 add_convert_fusion
  38.7 16.0 %all_to_all.10 = bf16[8,64,256]{2,1,0:T(8,128)(2,1)S(1)} all-to-all(bf16[8,64,256]{2,1,0:T(8,128)(2,1)S(1)} %bitcast.13), channel_id=1, replica_groups={{0,2,4,6,8,10,12,14},{1,3,5,7,9,11,13,15},{16,18,20,22,24,26,28,30},{17..., dimensions={0} | all-to-all | bytes 524288 | tf_op jit(solution)/shard_map/all_to_all | solution.py:331
  54.7 0.6 %broadcast_multiply_fusion = f32[64,256]{1,0:T(8,128)} fusion(f32[64,256]{1,0:T(8,128)S(1)} %convert_reduce_fusion), kind=kLoop, calls=%fused_computation.2 | loop fusion | flops 16384 | bytes 131072 | tf_op jit(solution)/shard_map/mul | solution.py:333
  (1 shorter events, 0.0 us)
Async XLA Ops:
  2.6 30.3 %all-to-all-start = ((bf16[16,128,256]{2,1,0:T(8,128)(2,1)}), bf16[16,128,256]{2,1,0:T(8,128)(2,1)S(1)}, u32[]{:S(2)}, u32[]{:S(2)}) async-start(bf16[16,128,256]{2,1,0:T(8,128)(2,1)} %get-tuple-element.11), calls=%async_computation | async-start | bytes 2097152 | tf_op jit(solution)/shard_map/all_to_all | solution.py:315
  10.0 25.6 %collective-permute-start = (bf16[3,128,256]{2,1,0:T(8,128)(2,1)}, bf16[3,128,256]{2,1,0:T(8,128)(2,1)S(1)}, u32[]{:S(2)}, u32[]{:S(2)}) collective-permute-start(bf16[3,128,256]{2,1,0:T(8,128)(2,1)} %get-tuple-element.12), channel_id=1, source_target_pairs={{0,1},{1,0},{2,3},{3,2},{4,5},{5,4},{6,7},{7,6},{8,9},{9,8},{10,11... | collective-permute-start | bytes 589832 | tf_op jit(solution)/shard_map/ppermute | solution.py:317
  10.4 25.2 %collective-permute-start.1 = (bf16[3,128,256]{2,1,0:T(8,128)(2,1)}, bf16[3,128,256]{2,1,0:T(8,128)(2,1)S(1)}, u32[]{:S(2)}, u32[]{:S(2)}) collective-permute-start(bf16[3,128,256]{2,1,0:T(8,128)(2,1)} %get-tuple-element.13), channel_id=1, source_target_pairs={{1,2},{2,1},{3,4},{4,3},{5,6},{6,5},{7,8},{8,7},{9,10},{10,9},{11,... | collective-permute-start | bytes 589832 | tf_op jit(solution)/shard_map/ppermute | solution.py:316
  33.0 2.0 %copy-start = (bf16[512,3328]{1,0:T(8,128)(2,1)S(1)}, bf16[512,3328]{1,0:T(8,128)(2,1)}, u32[]{:S(2)}) copy-start(bf16[512,3328]{1,0:T(8,128)(2,1)} %get-tuple-element.10.weights) | copy-start | bytes 10223620
  35.7 2.0 %copy-start.1 = (bf16[512,3328]{1,0:T(8,128)(2,1)S(1)}, bf16[512,3328]{1,0:T(8,128)(2,1)}, u32[]{:S(2)}) copy-start(bf16[512,3328]{1,0:T(8,128)(2,1)} %get-tuple-element.14.weights) | copy-start | bytes 10223620
  36.1 2.5 %collective-permute-start.2 = (f32[512,256]{1,0:T(8,128)S(1)}, f32[512,256]{1,0:T(8,128)S(1)}, u32[]{:S(2)}, u32[]{:S(2)}) collective-permute-start(f32[512,256]{1,0:T(8,128)S(1)} %near_kernel.1), channel_id=1, source_target_pairs={{0,1},{1,0},{2,3},{3,2},{4,5},{5,4},{6,7},{7,6},{8,9},{9,8},{10,11... | collective-permute-start | bytes 1572872 | tf_op jit(solution)/shard_map/ppermute | solution.py:326

commit v6 on v5

--- a/solution.py
+++ b/solution.py
@@ -53,9 +53,9 @@
 
 def project_kernel(parts, lent, middle, wide, share, pattern_in, counts_in, exponents_in, values_in, matrices, *refs):
     kept, terms, owned = pattern_in.shape
-    outs = refs[:2]
-    (acc, basis, turned, split, held, staged, partial, values, pattern, counts,
-     own_table, ghost_table, own_slots, ghost_slots, exponents, listed, came, read, moved, went) = refs[2:]
+    send_far, send_rest, keep_all = refs[:3]
+    (acc, basis, turned, split, held, staged_rest, staged_keep, partial, values, pattern, counts,
+     own_table, ghost_table, own_slots, ghost_slots, exponents, listed, came, read, moved, went) = refs[3:]
     me = lax.axis_index("dom")
     size = held.shape[-1]
     columns = values.shape[1]
@@ -194,32 +194,42 @@
         return pl.ds(pl.multiple_of((2 * m + side) * share, share), share)
 
     deep = ghosts * size
+    held_slots = send_far.shape[1] // size
+    distant = held_slots * size
     leaving = []
 
-    def leave(n, lanes):
-        leaving.append(pltpu.make_async_copy(staged.at[n, :, lanes], outs[n].at[:, lanes], went.at[len(leaving)]))
+    def leave(source, target, lanes):
+        leaving.append(pltpu.make_async_copy(source.at[:, lanes], target.at[:, lanes], went.at[len(leaving)]))
         leaving[-1].start()
 
-    sides = (1 - parity, parity)
-    for n, side in enumerate(sides):
+    def settle(side, first, last, place):
         for q in range(terms):
             for m in range(runs):
                 rows = pl.ds((q * runs + m) * share, share)
-                for g in range(ghosts):
-                    lanes = slice(g * size, (g + 1) * size)
-                    staged[n, rows, lanes] = acc[q * ghosts + g, run(m, side), :].astype(jnp.bfloat16)
-        leave(n, slice(0, deep))
-    lax.fori_loop(middle, steps, body, 0)
-    gather(steps - 1)
-    for n, side in enumerate(sides):
+                for g in range(first, last):
+                    lanes = slice((g - first) * size, (g - first + 1) * size)
+                    place[rows, lanes] = acc[q * ghosts + g, run(m, side), :].astype(jnp.bfloat16)
+
+    def settle_own(side, start, place):
         for q in range(terms):
             for m in range(runs):
                 exact = partial[pl.ds(pl.multiple_of(q * columns + (2 * m + side) * share, share), share), :]
                 upper = exact.astype(jnp.bfloat16)
                 rows = pl.ds((q * runs + m) * share, share)
-                staged[n, rows, deep:deep + columns] = upper
-                staged[n, rows, deep + columns:] = (exact - upper.astype(jnp.float32)).astype(jnp.bfloat16)
-        leave(n, slice(deep, deep + 2 * columns))
+                place[rows, start:start + columns] = upper
+                place[rows, start + columns:] = (exact - upper.astype(jnp.float32)).astype(jnp.bfloat16)
+
+    settle(parity, 0, ghosts, staged_keep)
+    leave(staged_keep, keep_all, slice(0, deep))
+    settle(1 - parity, held_slots, ghosts, staged_rest)
+    leave(staged_rest, send_rest, slice(0, deep - distant))
+    settle(1 - parity, 0, held_slots, send_far)
+    lax.fori_loop(middle, steps, body, 0)
+    gather(steps - 1)
+    settle_own(1 - parity, deep - distant, staged_rest)
+    leave(staged_rest, send_rest, slice(deep - distant, deep - distant + 2 * columns))
+    settle_own(parity, deep, staged_keep)
+    leave(staged_keep, keep_all, slice(deep, deep + 2 * columns))
     for copy in leaving:
         copy.wait()
 
@@ -229,22 +239,31 @@
     size = matrices.shape[-1]
     columns = values.shape[1]
     ghosts = parts + 2 * (lent - 1)
-    half = jax.ShapeDtypeStruct((terms * columns // 2, ghosts * size + 2 * columns), jnp.bfloat16)
+    half = lambda lanes: jax.ShapeDtypeStruct((terms * columns // 2, lanes), jnp.bfloat16)
+    held_slots = parts * 6 // 16
+    far = half(held_slots * size)
+    rest = half((ghosts - held_slots) * size + 2 * columns)
+    keep = half(ghosts * size + 2 * columns)
     wide = 8
+    rooms = [
+        ((terms * ghosts + 1, columns, size), jnp.float32),
+        ((owned + 1, size, columns), jnp.bfloat16),
+        ((owned, columns, size), jnp.bfloat16),
+        ((2, terms, 4 * size, columns), jnp.bfloat16),
+        (matrices.shape, jnp.bfloat16),
+        (rest.shape, rest.dtype),
+        (keep.shape, keep.dtype),
+        ((terms * columns, columns), jnp.float32),
+        (values.shape, values.dtype),
+    ]
+    needed = sum(math.prod(shape) * jnp.dtype(dtype).itemsize for shape, dtype in rooms)
+    grant = max(52 * 2**20, needed + 4 * 2**20)
     return pl.pallas_call(
         functools.partial(project_kernel, parts, lent, owned // 3, wide, terms * columns // parts),
-        out_shape=(half, half),
+        out_shape=(far, rest, keep),
         in_specs=[ANY] * 5,
-        out_specs=(ANY, ANY),
-        scratch_shapes=[
-            pltpu.VMEM((terms * ghosts + 1, columns, size), jnp.float32),
-            pltpu.VMEM((owned + 1, size, columns), jnp.bfloat16),
-            pltpu.VMEM((owned, columns, size), jnp.bfloat16),
-            pltpu.VMEM((2, terms, 4 * size, columns), jnp.bfloat16),
-            pltpu.VMEM(matrices.shape, jnp.bfloat16),
-            pltpu.VMEM((2,) + half.shape, half.dtype),
-            pltpu.VMEM((terms * columns, columns), jnp.float32),
-            pltpu.VMEM(values.shape, values.dtype),
+        out_specs=(VMEM, ANY, ANY),
+        scratch_shapes=[pltpu.VMEM(*room) for room in rooms] + [
             pltpu.VMEM(pattern.shape, jnp.int32),
             pltpu.VMEM(counts.shape, jnp.int32),
             pltpu.VMEM(pattern.shape, jnp.int32),
@@ -258,7 +277,7 @@
             pltpu.SemaphoreType.DMA((2,)),
             pltpu.SemaphoreType.DMA((4,)),
         ],
-        compiler_params=pltpu.CompilerParams(vmem_limit_bytes=60 * 2**20),
+        compiler_params=pltpu.CompilerParams(vmem_limit_bytes=grant),
         cost_estimate=pl.CostEstimate(
             flops=2 * matrices.size * columns, bytes_accessed=2 * matrices.size, transcendentals=0
         ),
@@ -266,40 +285,48 @@
     )(pattern, counts, exponents, values, matrices)
 
 
+def whole(ref):
+    columns = ref.shape[1] // 2
+    return ref[:, :columns].astype(jnp.float32) + ref[:, columns:].astype(jnp.float32)
+
+
 def far_kernel(weights, far, out):
-    columns = out.shape[1]
-    deep = weights.shape[1] - 2 * columns
-    total = weights[:, deep:deep + columns].astype(jnp.float32) + weights[:, deep + columns:].astype(jnp.float32)
-    out[...] = total + jnp.dot(weights[:, :far.shape[0]], far[...], preferred_element_type=jnp.float32)
-
-
-def near_kernel(weights, total, far, inner, outer, out):
-    start = far.shape[0]
-    middle = start + inner.shape[0]
-    stop = middle + outer.shape[0]
-    near = jnp.dot(weights[:, start:middle], inner[...], preferred_element_type=jnp.float32)
-    near += jnp.dot(weights[:, middle:stop], outer[...], preferred_element_type=jnp.float32)
-    out[...] = total[...] + near
+    out[...] = jnp.dot(weights[...], far[:weights.shape[1], :], preferred_element_type=jnp.float32)
+
+
+def near_kernel(done, total, weights, far, inner, outer, out):
+    result = total[...] + whole(weights.at[:, weights.shape[1] - 2 * out.shape[1]:])
+    start = 0
+    for block in (far.at[done:, :], inner, outer):
+        stop = start + block.shape[0]
+        result += jnp.dot(weights[:, start:stop], block[...], preferred_element_type=jnp.float32)
+        start = stop
+    out[...] = result
 
 
 def half_kernel(weights, far, inner, outer, out):
-    far_kernel(weights, far, out)
-    near_kernel(weights, out, far, inner, outer, out)
-
-
-def half_partial(kernel, weights, *blocks):
-    rows, columns = weights.shape[0], blocks[-1].shape[1]
+    total = whole(weights.at[:, weights.shape[1] - 2 * out.shape[1]:])
+    start = 0
+    for block in (far, inner, outer):
+        stop = start + block.shape[0]
+        total += jnp.dot(weights[:, start:stop], block[...], preferred_element_type=jnp.float32)
+        start = stop
+    out[...] = total
+
+
+def half_partial(name, kernel, *arrays):
+    rows, columns = arrays[0].shape[0], arrays[-1].shape[1]
     return pl.pallas_call(
         kernel,
         out_shape=jax.ShapeDtypeStruct((rows, columns), jnp.float32),
-        in_specs=[VMEM] * (1 + len(blocks)),
+        in_specs=[VMEM] * len(arrays),
         out_specs=VMEM,
         compiler_params=pltpu.CompilerParams(vmem_limit_bytes=4 * 2**20),
         cost_estimate=pl.CostEstimate(
-            flops=2 * weights.size * columns, bytes_accessed=2 * weights.size, transcendentals=0
+            flops=2 * rows * columns * 4096, bytes_accessed=sum(a.size * 2 for a in arrays), transcendentals=0
         ),
-        name=kernel.__name__,
-    )(weights, *blocks)
+        name=name,
+    )(*arrays)
 
 
 def on_device(matrices, values, exponents, pattern, block_counts, send_lists, ghost_counts):
@@ -316,15 +343,17 @@
     outer = lax.ppermute(outer, "dom", others)
     inner = lax.ppermute(inner, "dom", mates)
 
-    send_weights, keep_weights = project(
+    far_weights, rest_weights, weights = project(
         jnp.transpose(pattern, (2, 0, 1)), block_counts, exponents, values, matrices, parts, lent
     )
     flat = lambda a: a.reshape(-1, columns)
     far, inner, outer = flat(far), flat(inner), flat(outer)
-    send = half_partial(far_kernel, send_weights, far)
-    send = half_partial(near_kernel, send_weights, send, far, inner, outer)
+    send = half_partial("far", far_kernel, far_weights, far)
+    send = half_partial(
+        "near", functools.partial(near_kernel, far_weights.shape[1]), send, rest_weights, far, inner, outer
+    )
     came = lax.ppermute(send, "dom", mates)
-    both = came + half_partial(half_kernel, keep_weights, far, inner, outer)
+    both = came + half_partial("half", half_kernel, weights, far, inner, outer)
     share = terms * columns // parts
     both = both.astype(jnp.bfloat16).reshape(parts // 2, share, columns)
     groups = [list(range(core, parts, 2)) for core in range(2)]

time: 55.7 us -> 54.5 us (0.978)
  local copies, waits for them, and re-layouts: 2.8 us -> 1.34 us
  waiting for transfers between devices: 4.02 us -> 5.05 us
    unnamed x4 -> x10, local copies, waits for them, and re-layouts: 2.8 us -> 1.34 us
  transfers between devices with their start and end apart: 4 -> 4, of which waited for: 1 -> 2; matrix products, arithmetic and copies ran while one was open for 0% -> 0% of each run, Pallas kernels for 35% -> 34%
where the time goes in v6:
time: 54.5 us; the launch traced here: 54.2 us
  Pallas kernels  22.1 us (41%)
  blocking collectives  15.7 us (29%)
  starting transfers between devices  9.13 us (17%)
  waiting for transfers between devices  5.05 us (9%)
  local copies, waits for them, and re-layouts  1.34 us (2%)
  other arithmetic  0.75 us (1%)
    pallas_call x1, Pallas kernels, project(): pl.pallas_call(functools.partial(project_kernel, parts, lent, owned // 3,...  17.3 us
    all_to_all x1, blocking collectives, on_device(): lax.all_to_all(both, 'dom', split_axis=0, concat_axis=0, tiled=True, axis...  15.7 us
    all_to_all x1, starting transfers between devices, on_device(): far = lax.all_to_all(far, 'dom', split_axis=0, concat_axis=0, tiled=True)  7.39 us
    all_to_all x1, waiting for transfers between devices, on_device(): far = lax.all_to_all(far, 'dom', split_axis=0, concat_axis=0, tiled=True)  4.49 us
    pallas_call x1, Pallas kernels, pack(): pl.pallas_call(functools.partial(pack_kernel, parts, size), out_shape=(bl...  2.68 us
    pallas_call x3, Pallas kernels, half_partial(): pl.pallas_call(kernel, out_shape=jax.ShapeDtypeStruct((rows, columns), jn...  2.12 us
    unnamed x10, local copies, waits for them, and re-layouts  1.34 us
  transfers between devices with their start and end apart: 4, of which 2 were waited for; matrix products, arithmetic and copies ran while one was open for 0% of the time, Pallas kernels for 34%

profile of v6, /device:TPU:0, one launch (start us, length us, event | category | flops | bytes accessed | tf_op | source)
XLA Modules:
  0.0 54.2 jit_solution(17296950093500612611)
XLA Ops:
  0.0 0.0 copy-start.3
  0.0 0.0 copy-start.4
  0.0 0.0 copy-start.2
  0.0 2.7 %pack.1 = (bf16[16,128,256]{2,1,0:T(8,128)(2,1)}, bf16[3,128,256]{2,1,0:T(8,128)(2,1)}, bf16[3,128,256]{2,1,0:T(8,128)(2,1)}) custom-call(s32[1,4,16]{2,1,0:T(4,128)} %bitcast.15, s32[24]{0:T(128)} %exponents.1, bf16[3072,256]{1,0:T(8,128)(2,1)} %values.1), custom_call_target="tpu_custom_call" | custom-call | tf_op jit(solution)/shard_map/pack/pallas_call | solution.py:45
  2.7 7.4 %all-to-all-start = ((bf16[16,128,256]{2,1,0:T(8,128)(2,1)}), bf16[16,128,256]{2,1,0:T(8,128)(2,1)S(1)}, u32[]{:S(2)}, u32[]{:S(2)}) async-start(bf16[16,128,256]{2,1,0:T(8,128)(2,1)} %get-tuple-element.12), calls=%async_computation | async-start | bytes 2097152 | tf_op jit(solution)/shard_map/all_to_all | solution.py:342
  10.1 0.4 collective-permute-start
  10.5 0.7 %collective-permute-start.1 = (bf16[3,128,256]{2,1,0:T(8,128)(2,1)}, bf16[3,128,256]{2,1,0:T(8,128)(2,1)S(1)}, u32[]{:S(2)}, u32[]{:S(2)}) collective-permute-start(bf16[3,128,256]{2,1,0:T(8,128)(2,1)} %get-tuple-element.15), channel_id=1, source_target_pairs={{1,2},{2,1},{3,4},{4,3},{5,6},{6,5},{7,8},{8,7},{9,10},{10,9},{11,... | collective-permute-start | bytes 589832 | tf_op jit(solution)/shard_map/ppermute | solution.py:343
  11.2 0.0 copy-done.3
  11.2 0.0 copy-done.4
  11.2 0.0 copy-done.2
  11.2 17.3 %project.1 = (bf16[512,768]{1,0:T(8,128)(2,1)S(1)}, bf16[512,2560]{1,0:T(8,128)(2,1)}, bf16[512,3328]{1,0:T(8,128)(2,1)}) custom-call(s32[6,4,24]{2,1,0:T(4,128)S(1)} %bitcast.13, s32[4,24]{1,0:T(4,128)S(1)} %copy-done.4, s32[24]{0:T(128)S(1)} %copy-done.3, bf16[3072,256]{1,0:T(8,128)(2,1)} %values.1, bf16[4,24,6,128,128]{4,3,2,1,0:T(8,128)(2,1)} %matrices.1), custom_call_target="tpu_custom_call" | custom-call | flops 4831838208 | bytes 18874368 | tf_op jit(solution)/shard_map/project/pallas_call | solution.py:261
  28.5 4.5 %all-to-all-done = bf16[16,128,256]{2,1,0:T(8,128)(2,1)S(1)} async-done(((bf16[16,128,256]{2,1,0:T(8,128)(2,1)}), bf16[16,128,256]{2,1,0:T(8,128)(2,1)S(1)}, u32[]{:S(2)}, u32[]{:S(2)}) %all-to-all-start) | async-done | bytes 1048608 | tf_op jit(solution)/shard_map/all_to_all | solution.py:342
  33.0 0.0 copy-start.1
  33.0 0.4 far.1.total
  33.4 0.0 copy-start
  33.4 0.0 collective-permute-done
  33.4 0.0 collective-permute-done.1
  33.4 1.3 %copy-done.1 = bf16[512,2560]{1,0:T(8,128)(2,1)S(1)} copy-done((bf16[512,2560]{1,0:T(8,128)(2,1)S(1)}, bf16[512,2560]{1,0:T(8,128)(2,1)}, u32[]{:S(2)}) %copy-start.1) | copy-done | bytes 2621464
  34.8 0.8 %near.1 = f32[512,256]{1,0:T(8,128)S(1)} custom-call(f32[512,256]{1,0:T(8,128)S(1)} %far.1.total, bf16[512,2560]{1,0:T(8,128)(2,1)S(1)} %copy-done.1, bf16[2048,256]{1,0:T(8,128)(2,1)S(1)} %bitcast.7, bf16[384,256]{1,0:T(8,128)(2,1)S(1)} %bitcast.9, bf16[384,256]{1,0:T(8,128)(2,1)S(1)} %bitcast.11), custom_call_target="tpu_custom_call" | custom-call | flops 1073741824 | bytes 4325376 | tf_op jit(solution)/shard_map/near/pallas_call | solution.py:319
  35.5 0.7 %collective-permute-start.2 = (f32[512,256]{1,0:T(8,128)S(1)}, f32[512,256]{1,0:T(8,128)S(1)}, u32[]{:S(2)}, u32[]{:S(2)}) collective-permute-start(f32[512,256]{1,0:T(8,128)S(1)} %near.1), channel_id=1, source_target_pairs={{0,1},{1,0},{2,3},{3,2},{4,5},{5,4},{6,7},{7,6},{8,9},{9,8},{10,11... | collective-permute-start | bytes 1572872 | tf_op jit(solution)/shard_map/ppermute | solution.py:355
  36.2 0.0 copy-done
  36.2 1.0 %half.1 = f32[512,256]{1,0:T(8,128)S(1)} custom-call(bf16[512,3328]{1,0:T(8,128)(2,1)S(1)} %copy-done, bf16[2048,256]{1,0:T(8,128)(2,1)S(1)} %bitcast.8, bf16[384,256]{1,0:T(8,128)(2,1)S(1)} %bitcast.10, bf16[384,256]{1,0:T(8,128)(2,1)S(1)} %bitcast.12), custom_call_target="tpu_custom_call" | custom-call | flops 1073741824 | bytes 4849664 | tf_op jit(solution)/shard_map/half/pallas_call | solution.py:319
  37.2 0.6 %collective-permute-done.2 = f32[512,256]{1,0:T(8,128)S(1)} collective-permute-done((f32[512,256]{1,0:T(8,128)S(1)}, f32[512,256]{1,0:T(8,128)S(1)}, u32[]{:S(2)}, u32[]{:S(2)}) %collective-permute-start.2) | collective-permute-done | bytes 524320 | tf_op jit(solution)/shard_map/ppermute | solution.py:355
  37.8 0.1 add_convert_fusion
  37.8 15.7 %all_to_all.10 = bf16[8,64,256]{2,1,0:T(8,128)(2,1)S(1)} all-to-all(bf16[8,64,256]{2,1,0:T(8,128)(2,1)S(1)} %bitcast.14), channel_id=1, replica_groups={{0,2,4,6,8,10,12,14},{1,3,5,7,9,11,13,15},{16,18,20,22,24,26,28,30},{17..., dimensions={0} | all-to-all | bytes 524288 | tf_op jit(solution)/shard_map/all_to_all | solution.py:360
  53.6 0.6 %broadcast_multiply_fusion = f32[64,256]{1,0:T(8,128)} fusion(f32[64,256]{1,0:T(8,128)S(1)} %convert_reduce_fusion), kind=kLoop, calls=%fused_computation.2 | loop fusion | flops 16384 | bytes 131072 | tf_op jit(solution)/shard_map/mul | solution.py:362
  (1 shorter events, 0.0 us)
Async XLA Ops:
  0.0 11.2 %copy-start.3 = (s32[24]{0:T(128)S(1)}, s32[24]{0:T(128)}, u32[]{:S(2)}) copy-start(s32[24]{0:T(128)} %exponents.1) | copy-start | bytes 292
  0.0 11.2 %copy-start.4 = (s32[4,24]{1,0:T(4,128)S(1)}, s32[4,24]{1,0:T(4,128)}, u32[]{:S(2)}) copy-start(s32[4,24]{1,0:T(4,128)} %counts_in.1) | copy-start | bytes 1156
  0.0 11.2 %copy-start.2 = (s32[4,24,6]{1,0,2:T(4,128)S(1)}, s32[4,24,6]{1,0,2:T(4,128)}, u32[]{:S(2)}) copy-start(s32[4,24,6]{1,0,2:T(4,128)} %param.10) | copy-start | bytes 6916
  2.7 30.3 %all-to-all-start = ((bf16[16,128,256]{2,1,0:T(8,128)(2,1)}), bf16[16,128,256]{2,1,0:T(8,128)(2,1)S(1)}, u32[]{:S(2)}, u32[]{:S(2)}) async-start(bf16[16,128,256]{2,1,0:T(8,128)(2,1)} %get-tuple-element.12), calls=%async_computation | async-start | bytes 2097152 | tf_op jit(solution)/shard_map/all_to_all | solution.py:342
  10.1 23.3 %collective-permute-start = (bf16[3,128,256]{2,1,0:T(8,128)(2,1)}, bf16[3,128,256]{2,1,0:T(8,128)(2,1)S(1)}, u32[]{:S(2)}, u32[]{:S(2)}) collective-permute-start(bf16[3,128,256]{2,1,0:T(8,128)(2,1)} %get-tuple-element.14), channel_id=1, source_target_pairs={{0,1},{1,0},{2,3},{3,2},{4,5},{5,4},{6,7},{7,6},{8,9},{9,8},{10,11... | collective-permute-start | bytes 589832 | tf_op jit(solution)/shard_map/ppermute | solution.py:344
  10.5 22.9 %collective-permute-start.1 = (bf16[3,128,256]{2,1,0:T(8,128)(2,1)}, bf16[3,128,256]{2,1,0:T(8,128)(2,1)S(1)}, u32[]{:S(2)}, u32[]{:S(2)}) collective-permute-start(bf16[3,128,256]{2,1,0:T(8,128)(2,1)} %get-tuple-element.15), channel_id=1, source_target_pairs={{1,2},{2,1},{3,4},{4,3},{5,6},{6,5},{7,8},{8,7},{9,10},{10,9},{11,... | collective-permute-start | bytes 589832 | tf_op jit(solution)/shard_map/ppermute | solution.py:343
  33.0 1.7 %copy-start.1 = (bf16[512,2560]{1,0:T(8,128)(2,1)S(1)}, bf16[512,2560]{1,0:T(8,128)(2,1)}, u32[]{:S(2)}) copy-start(bf16[512,2560]{1,0:T(8,128)(2,1)} %get-tuple-element.13.weights) | copy-start | bytes 7864324
  33.4 2.8 %copy-start = (bf16[512,3328]{1,0:T(8,128)(2,1)S(1)}, bf16[512,3328]{1,0:T(8,128)(2,1)}, u32[]{:S(2)}) copy-start(bf16[512,3328]{1,0:T(8,128)(2,1)} %get-tuple-element.16.weights) | copy-start | bytes 10223620
  35.5 2.2 %collective-permute-start.2 = (f32[512,256]{1,0:T(8,128)S(1)}, f32[512,256]{1,0:T(8,128)S(1)}, u32[]{:S(2)}, u32[]{:S(2)}) collective-permute-start(f32[512,256]{1,0:T(8,128)S(1)} %near.1), channel_id=1, source_target_pairs={{0,1},{1,0},{2,3},{3,2},{4,5},{5,4},{6,7},{7,6},{8,9},{9,8},{10,11... | collective-permute-start | bytes 1572872 | tf_op jit(solution)/shard_map/ppermute | solution.py:355

commit v7 on v6

--- a/solution.py
+++ b/solution.py
@@ -341,11 +341,12 @@
     others = [(p, q) for n in range(1, parts - 1, 2) for p, q in ((n, n + 1), (n + 1, n))]
     far = lax.all_to_all(far, "dom", split_axis=0, concat_axis=0, tiled=True)
     outer = lax.ppermute(outer, "dom", others)
-    inner = lax.ppermute(inner, "dom", mates)
 
     far_weights, rest_weights, weights = project(
         jnp.transpose(pattern, (2, 0, 1)), block_counts, exponents, values, matrices, parts, lent
     )
+    inner, far_weights, rest_weights, weights = lax.optimization_barrier((inner, far_weights, rest_weights, weights))
+    inner = lax.ppermute(inner, "dom", mates)
     flat = lambda a: a.reshape(-1, columns)
     far, inner, outer = flat(far), flat(inner), flat(outer)
     send = half_partial("far", far_kernel, far_weights, far)

time: 54.5 us -> 54.5 us (level)
  starting transfers between devices: 9.13 us -> 13.6 us
  waiting for transfers between devices: 5.05 us -> 1.33 us
    ppermute x1, starting transfers between devices: 0.41 us -> 5.35 us  [on_device(): inner = lax.ppermute(inner, 'dom', mates)]
    all_to_all x1, waiting for transfers between devices: 4.49 us -> 0.01 us  [on_device(): far = lax.all_to_all(far, 'dom', split_axis=0, concat_axis=0, tiled=True)]
    ppermute x1, waiting for transfers between devices: 0.01 us -> 0.67 us  [on_device(): inner = lax.ppermute(inner, 'dom', mates)]
    unnamed x10 -> x12, local copies, waits for them, and re-layouts: 1.34 us -> 0.84 us
where the time goes in v7:
time: 54.5 us; the launch traced here: 54.2 us
  Pallas kernels  22.1 us (41%)
  blocking collectives  15.5 us (28%)
  starting transfers between devices  13.6 us (25%)
  waiting for transfers between devices  1.33 us (2%)
  local copies, waits for them, and re-layouts  0.84 us (2%)
  other arithmetic  0.75 us (1%)
    pallas_call x1, Pallas kernels, project(): pl.pallas_call(functools.partial(project_kernel, parts, lent, owned // 3,...  17.3 us
    all_to_all x1, blocking collectives, on_device(): lax.all_to_all(both, 'dom', split_axis=0, concat_axis=0, tiled=True, axis...  15.5 us
    all_to_all x1, starting transfers between devices, on_device(): far = lax.all_to_all(far, 'dom', split_axis=0, concat_axis=0, tiled=True)  7.39 us
    ppermute x1, starting transfers between devices, on_device(): inner = lax.ppermute(inner, 'dom', mates)  5.35 us
    pallas_call x1, Pallas kernels, pack(): pl.pallas_call(functools.partial(pack_kernel, parts, size), out_shape=(bl...  2.68 us
    pallas_call x3, Pallas kernels, half_partial(): pl.pallas_call(kernel, out_shape=jax.ShapeDtypeStruct((rows, columns), jn...  2.12 us
  transfers between devices with their start and end apart: 4, of which 2 were waited for; matrix products, arithmetic and copies ran while one was open for 0% of the time, Pallas kernels for 34%

profile of v7, /device:TPU:0, one launch (start us, length us, event | category | flops | bytes accessed | tf_op | source)
XLA Modules:
  0.0 54.2 jit_solution(1010428892962169132)
XLA Ops:
  0.0 0.0 copy-start.3
  0.0 0.0 copy-start.4
  0.0 0.0 copy-start.2
  0.0 2.7 %pack.1 = (bf16[16,128,256]{2,1,0:T(8,128)(2,1)}, bf16[3,128,256]{2,1,0:T(8,128)(2,1)}, bf16[3,128,256]{2,1,0:T(8,128)(2,1)}) custom-call(s32[1,4,16]{2,1,0:T(4,128)} %bitcast.15, s32[24]{0:T(128)} %exponents_in.1, bf16[3072,256]{1,0:T(8,128)(2,1)} %values_in.1), custom_call_target="tpu_custom_call" | custom-call | tf_op jit(solution)/shard_map/pack/pallas_call | solution.py:45
  2.7 7.4 %all-to-all-start = ((bf16[16,128,256]{2,1,0:T(8,128)(2,1)}), bf16[16,128,256]{2,1,0:T(8,128)(2,1)S(1)}, u32[]{:S(2)}, u32[]{:S(2)}) async-start(bf16[16,128,256]{2,1,0:T(8,128)(2,1)} %get-tuple-element.20), calls=%async_computation | async-start | bytes 2097152 | tf_op jit(solution)/shard_map/all_to_all | solution.py:342
  10.1 0.7 %collective-permute-start.1 = (bf16[3,128,256]{2,1,0:T(8,128)(2,1)}, bf16[3,128,256]{2,1,0:T(8,128)(2,1)S(1)}, u32[]{:S(2)}, u32[]{:S(2)}) collective-permute-start(bf16[3,128,256]{2,1,0:T(8,128)(2,1)} %get-tuple-element.23), channel_id=1, source_target_pairs={{1,2},{2,1},{3,4},{4,3},{5,6},{6,5},{7,8},{8,7},{9,10},{10,9},{11,... | collective-permute-start | bytes 589832 | tf_op jit(solution)/shard_map/ppermute | solution.py:343
  10.8 0.0 copy-done.3
  10.8 0.0 copy-done.4
  10.8 0.0 copy-done.2
  10.8 0.0 copy-start.5
  10.8 17.3 %project.1 = (bf16[512,768]{1,0:T(8,128)(2,1)S(1)}, bf16[512,2560]{1,0:T(8,128)(2,1)}, bf16[512,3328]{1,0:T(8,128)(2,1)}) custom-call(s32[6,4,24]{2,1,0:T(4,128)S(1)} %bitcast.13, s32[4,24]{1,0:T(4,128)S(1)} %copy-done.4, s32[24]{0:T(128)S(1)} %copy-done.3, bf16[3072,256]{1,0:T(8,128)(2,1)} %values_in.1, bf16[4,24,6,128,128]{4,3,2,1,0:T(8,128)(2,1)} %matrices.1), custom_call_target="tpu_custom_call" | custom-call | flops 4831838208 | bytes 18874368 | tf_op jit(solution)/shard_map/project/pallas_call | solution.py:261
  28.1 0.0 copy-done.5
  28.2 5.3 %collective-permute-start = (bf16[3,128,256]{2,1,0:T(8,128)(2,1)S(1)}, bf16[3,128,256]{2,1,0:T(8,128)(2,1)S(1)}, u32[]{:S(2)}, u32[]{:S(2)}) collective-permute-start(bf16[3,128,256]{2,1,0:T(8,128)(2,1)S(1)} %copy-done.5), channel_id=1, source_target_pairs={{0,1},{1,0},{2,3},{3,2},{4,5},{5,4},{6,7},{7,6},{8,9},{9,8},{10,11... | collective-permute-start | bytes 589832 | tf_op jit(solution)/shard_map/ppermute | solution.py:349
  33.5 0.0 all-to-all-done
  33.5 0.0 copy-start.1
  33.5 0.4 far.1.total
  33.9 0.0 copy-start
  33.9 0.0 collective-permute-done.1
  33.9 0.7 %collective-permute-done = bf16[3,128,256]{2,1,0:T(8,128)(2,1)S(1)} collective-permute-done((bf16[3,128,256]{2,1,0:T(8,128)(2,1)S(1)}, bf16[3,128,256]{2,1,0:T(8,128)(2,1)S(1)}, u32[]{:S(2)}, u32[]{:S(2)}) %collective-permute-start) | collective-permute-done | bytes 196640 | tf_op jit(solution)/shard_map/ppermute | solution.py:349
  34.6 0.7 %copy-done.1 = bf16[512,2560]{1,0:T(8,128)(2,1)S(1)} copy-done((bf16[512,2560]{1,0:T(8,128)(2,1)S(1)}, bf16[512,2560]{1,0:T(8,128)(2,1)}, u32[]{:S(2)}) %copy-start.1) | copy-done | bytes 2621464
  35.3 0.8 %near.1 = f32[512,256]{1,0:T(8,128)S(1)} custom-call(f32[512,256]{1,0:T(8,128)S(1)} %far.1.total, bf16[512,2560]{1,0:T(8,128)(2,1)S(1)} %copy-done.1, bf16[2048,256]{1,0:T(8,128)(2,1)S(1)} %bitcast.7, bf16[384,256]{1,0:T(8,128)(2,1)S(1)} %bitcast.11, bf16[384,256]{1,0:T(8,128)(2,1)S(1)} %bitcast.9), custom_call_target="tpu_custom_call" | custom-call | flops 1073741824 | bytes 4325376 | tf_op jit(solution)/shard_map/near/pallas_call | solution.py:319
  36.0 0.2 collective-permute-start.2
  36.2 0.2 copy-done
  36.4 1.0 %half.1 = f32[512,256]{1,0:T(8,128)S(1)} custom-call(bf16[512,3328]{1,0:T(8,128)(2,1)S(1)} %copy-done, bf16[2048,256]{1,0:T(8,128)(2,1)S(1)} %bitcast.8, bf16[384,256]{1,0:T(8,128)(2,1)S(1)} %bitcast.12, bf16[384,256]{1,0:T(8,128)(2,1)S(1)} %bitcast.10), custom_call_target="tpu_custom_call" | custom-call | flops 1073741824 | bytes 4849664 | tf_op jit(solution)/shard_map/half/pallas_call | solution.py:319
  37.3 0.7 %collective-permute-done.2 = f32[512,256]{1,0:T(8,128)S(1)} collective-permute-done((f32[512,256]{1,0:T(8,128)S(1)}, f32[512,256]{1,0:T(8,128)S(1)}, u32[]{:S(2)}, u32[]{:S(2)}) %collective-permute-start.2) | collective-permute-done | bytes 524320 | tf_op jit(solution)/shard_map/ppermute | solution.py:356
  38.0 0.1 add_convert_fusion
  38.1 15.5 %all_to_all.10 = bf16[8,64,256]{2,1,0:T(8,128)(2,1)S(1)} all-to-all(bf16[8,64,256]{2,1,0:T(8,128)(2,1)S(1)} %bitcast.14), channel_id=1, replica_groups={{0,2,4,6,8,10,12,14},{1,3,5,7,9,11,13,15},{16,18,20,22,24,26,28,30},{17..., dimensions={0} | all-to-all | bytes 524288 | tf_op jit(solution)/shard_map/all_to_all | solution.py:361
  53.6 0.6 %broadcast_multiply_fusion = f32[64,256]{1,0:T(8,128)} fusion(f32[64,256]{1,0:T(8,128)S(1)} %convert_reduce_fusion), kind=kLoop, calls=%fused_computation.2 | loop fusion | flops 16384 | bytes 131072 | tf_op jit(solution)/shard_map/mul | solution.py:363
  (1 shorter events, 0.0 us)
Async XLA Ops:
  0.0 10.8 %copy-start.3 = (s32[24]{0:T(128)S(1)}, s32[24]{0:T(128)}, u32[]{:S(2)}) copy-start(s32[24]{0:T(128)} %exponents_in.1) | copy-start | bytes 292
  0.0 10.8 %copy-start.4 = (s32[4,24]{1,0:T(4,128)S(1)}, s32[4,24]{1,0:T(4,128)}, u32[]{:S(2)}) copy-start(s32[4,24]{1,0:T(4,128)} %counts_in.1) | copy-start | bytes 1156
  0.0 10.8 %copy-start.2 = (s32[4,24,6]{1,0,2:T(4,128)S(1)}, s32[4,24,6]{1,0,2:T(4,128)}, u32[]{:S(2)}) copy-start(s32[4,24,6]{1,0,2:T(4,128)} %param.10) | copy-start | bytes 6916
  2.7 30.8 %all-to-all-start = ((bf16[16,128,256]{2,1,0:T(8,128)(2,1)}), bf16[16,128,256]{2,1,0:T(8,128)(2,1)S(1)}, u32[]{:S(2)}, u32[]{:S(2)}) async-start(bf16[16,128,256]{2,1,0:T(8,128)(2,1)} %get-tuple-element.20), calls=%async_computation | async-start | bytes 2097152 | tf_op jit(solution)/shard_map/all_to_all | solution.py:342
  10.1 23.8 %collective-permute-start.1 = (bf16[3,128,256]{2,1,0:T(8,128)(2,1)}, bf16[3,128,256]{2,1,0:T(8,128)(2,1)S(1)}, u32[]{:S(2)}, u32[]{:S(2)}) collective-permute-start(bf16[3,128,256]{2,1,0:T(8,128)(2,1)} %get-tuple-element.23), channel_id=1, source_target_pairs={{1,2},{2,1},{3,4},{4,3},{5,6},{6,5},{7,8},{8,7},{9,10},{10,9},{11,... | collective-permute-start | bytes 589832 | tf_op jit(solution)/shard_map/ppermute | solution.py:343
  10.8 17.4 %copy-start.5 = (bf16[3,128,256]{2,1,0:T(8,128)(2,1)S(1)}, bf16[3,128,256]{2,1,0:T(8,128)(2,1)}, u32[]{:S(2)}) copy-start(bf16[3,128,256]{2,1,0:T(8,128)(2,1)} %get-tuple-element.22) | copy-start | bytes 589828
  28.2 6.4 %collective-permute-start = (bf16[3,128,256]{2,1,0:T(8,128)(2,1)S(1)}, bf16[3,128,256]{2,1,0:T(8,128)(2,1)S(1)}, u32[]{:S(2)}, u32[]{:S(2)}) collective-permute-start(bf16[3,128,256]{2,1,0:T(8,128)(2,1)S(1)} %copy-done.5), channel_id=1, source_target_pairs={{0,1},{1,0},{2,3},{3,2},{4,5},{5,4},{6,7},{7,6},{8,9},{9,8},{10,11... | collective-permute-start | bytes 589832 | tf_op jit(solution)/shard_map/ppermute | solution.py:349
  33.5 1.7 %copy-start.1 = (bf16[512,2560]{1,0:T(8,128)(2,1)S(1)}, bf16[512,2560]{1,0:T(8,128)(2,1)}, u32[]{:S(2)}) copy-start(bf16[512,2560]{1,0:T(8,128)(2,1)} %get-tuple-element.21.weights) | copy-start | bytes 7864324
  33.9 2.5 %copy-start = (bf16[512,3328]{1,0:T(8,128)(2,1)S(1)}, bf16[512,3328]{1,0:T(8,128)(2,1)}, u32[]{:S(2)}) copy-start(bf16[512,3328]{1,0:T(8,128)(2,1)} %get-tuple-element.24.weights) | copy-start | bytes 10223620
  36.0 2.0 %collective-permute-start.2 = (f32[512,256]{1,0:T(8,128)S(1)}, f32[512,256]{1,0:T(8,128)S(1)}, u32[]{:S(2)}, u32[]{:S(2)}) collective-permute-start(f32[512,256]{1,0:T(8,128)S(1)} %near.1), channel_id=1, source_target_pairs={{0,1},{1,0},{2,3},{3,2},{4,5},{5,4},{6,7},{7,6},{8,9},{9,8},{10,11... | collective-permute-start | bytes 1572872 | tf_op jit(solution)/shard_map/ppermute | solution.py:356

commit v8 on v6

--- a/solution.py
+++ b/solution.py
@@ -355,11 +355,12 @@
     came = lax.ppermute(send, "dom", mates)
     both = came + half_partial("half", half_kernel, weights, far, inner, outer)
     share = terms * columns // parts
+    both = both * (1.0 / math.sqrt(row_count * parts))
     both = both.astype(jnp.bfloat16).reshape(parts // 2, share, columns)
     groups = [list(range(core, parts, 2)) for core in range(2)]
     pieces = lax.all_to_all(both, "dom", split_axis=0, concat_axis=0, tiled=True, axis_index_groups=groups)
     summed = jnp.sum(pieces.astype(jnp.float32), axis=0)
-    return summed * (1.0 / math.sqrt(row_count * parts))
+    return summed
 
 
 def solution(mesh):

time: 54.5 us -> 54.5 us (level)
    mul x1 -> x0, other arithmetic: 0.64 us -> none  [on_device(): return summed * (1.0 / math.sqrt(row_count * parts))]
    reduce_sum x1, other arithmetic: 0.04 us -> 0.67 us  [on_device(): summed = jnp.sum(pieces.astype(jnp.float32), axis=0)]
  transfers between devices with their start and end apart: 4 -> 4, of which waited for: 2 -> 2; matrix products, arithmetic and copies ran while one was open for 0% -> 0% of each run, Pallas kernels for 34% -> 35%
where the time goes in v8:
time: 54.5 us; the launch traced here: 54.2 us
  Pallas kernels  22.6 us (41%)
  blocking collectives  15.7 us (29%)
  starting transfers between devices  9.13 us (17%)
  waiting for transfers between devices  4.55 us (8%)
  local copies, waits for them, and re-layouts  1.34 us (2%)
  other arithmetic  0.74 us (1%)
    pallas_call x1, Pallas kernels, project(): pl.pallas_call(functools.partial(project_kernel, parts, lent, owned // 3,...  17.8 us
    all_to_all x1, blocking collectives, on_device(): lax.all_to_all(both, 'dom', split_axis=0, concat_axis=0, tiled=True, axis...  15.7 us
    all_to_all x1, starting transfers between devices, on_device(): far = lax.all_to_all(far, 'dom', split_axis=0, concat_axis=0, tiled=True)  7.39 us
    all_to_all x1, waiting for transfers between devices, on_device(): far = lax.all_to_all(far, 'dom', split_axis=0, concat_axis=0, tiled=True)  3.99 us
    pallas_call x1, Pallas kernels, pack(): pl.pallas_call(functools.partial(pack_kernel, parts, size), out_shape=(bl...  2.68 us
    pallas_call x3, Pallas kernels, half_partial(): pl.pallas_call(kernel, out_shape=jax.ShapeDtypeStruct((rows, columns), jn...  2.12 us
    unnamed x10, local copies, waits for them, and re-layouts  1.34 us
  transfers between devices with their start and end apart: 4, of which 2 were waited for; matrix products, arithmetic and copies ran while one was open for 0% of the time, Pallas kernels for 35%

profile of v8, /device:TPU:0, one launch (start us, length us, event | category | flops | bytes accessed | tf_op | source)
XLA Modules:
  0.0 54.2 jit_solution(12284040001915439719)
XLA Ops:
  0.0 0.0 copy-start.3
  0.0 0.0 copy-start.4
  0.0 0.0 copy-start.2
  0.0 2.7 %pack.1 = (bf16[16,128,256]{2,1,0:T(8,128)(2,1)}, bf16[3,128,256]{2,1,0:T(8,128)(2,1)}, bf16[3,128,256]{2,1,0:T(8,128)(2,1)}) custom-call(s32[1,4,16]{2,1,0:T(4,128)} %bitcast.15, s32[24]{0:T(128)} %exponents.1, bf16[3072,256]{1,0:T(8,128)(2,1)} %values.1), custom_call_target="tpu_custom_call" | custom-call | tf_op jit(solution)/shard_map/pack/pallas_call | solution.py:45
  2.7 7.4 %all-to-all-start = ((bf16[16,128,256]{2,1,0:T(8,128)(2,1)}), bf16[16,128,256]{2,1,0:T(8,128)(2,1)S(1)}, u32[]{:S(2)}, u32[]{:S(2)}) async-start(bf16[16,128,256]{2,1,0:T(8,128)(2,1)} %get-tuple-element.12), calls=%async_computation | async-start | bytes 2097152 | tf_op jit(solution)/shard_map/all_to_all | solution.py:342
  10.1 0.4 collective-permute-start
  10.5 0.7 %collective-permute-start.1 = (bf16[3,128,256]{2,1,0:T(8,128)(2,1)}, bf16[3,128,256]{2,1,0:T(8,128)(2,1)S(1)}, u32[]{:S(2)}, u32[]{:S(2)}) collective-permute-start(bf16[3,128,256]{2,1,0:T(8,128)(2,1)} %get-tuple-element.15), channel_id=1, source_target_pairs={{1,2},{2,1},{3,4},{4,3},{5,6},{6,5},{7,8},{8,7},{9,10},{10,9},{11,... | collective-permute-start | bytes 589832 | tf_op jit(solution)/shard_map/ppermute | solution.py:343
  11.2 0.0 copy-done.3
  11.2 0.0 copy-done.4
  11.2 0.0 copy-done.2
  11.2 17.8 %project.1 = (bf16[512,768]{1,0:T(8,128)(2,1)S(1)}, bf16[512,2560]{1,0:T(8,128)(2,1)}, bf16[512,3328]{1,0:T(8,128)(2,1)}) custom-call(s32[6,4,24]{2,1,0:T(4,128)S(1)} %bitcast.13, s32[4,24]{1,0:T(4,128)S(1)} %copy-done.4, s32[24]{0:T(128)S(1)} %copy-done.3, bf16[3072,256]{1,0:T(8,128)(2,1)} %values.1, bf16[4,24,6,128,128]{4,3,2,1,0:T(8,128)(2,1)} %matrices.1), custom_call_target="tpu_custom_call" | custom-call | flops 4831838208 | bytes 18874368 | tf_op jit(solution)/shard_map/project/pallas_call | solution.py:261
  29.0 4.0 %all-to-all-done = bf16[16,128,256]{2,1,0:T(8,128)(2,1)S(1)} async-done(((bf16[16,128,256]{2,1,0:T(8,128)(2,1)}), bf16[16,128,256]{2,1,0:T(8,128)(2,1)S(1)}, u32[]{:S(2)}, u32[]{:S(2)}) %all-to-all-start) | async-done | bytes 1048608 | tf_op jit(solution)/shard_map/all_to_all | solution.py:342
  33.0 0.0 copy-start.1
  33.0 0.4 far.1.total
  33.4 0.0 copy-start
  33.4 0.0 collective-permute-done
  33.4 0.0 collective-permute-done.1
  33.4 1.3 %copy-done.1 = bf16[512,2560]{1,0:T(8,128)(2,1)S(1)} copy-done((bf16[512,2560]{1,0:T(8,128)(2,1)S(1)}, bf16[512,2560]{1,0:T(8,128)(2,1)}, u32[]{:S(2)}) %copy-start.1) | copy-done | bytes 2621464
  34.8 0.8 %near.1 = f32[512,256]{1,0:T(8,128)S(1)} custom-call(f32[512,256]{1,0:T(8,128)S(1)} %far.1.total, bf16[512,2560]{1,0:T(8,128)(2,1)S(1)} %copy-done.1, bf16[2048,256]{1,0:T(8,128)(2,1)S(1)} %bitcast.7, bf16[384,256]{1,0:T(8,128)(2,1)S(1)} %bitcast.9, bf16[384,256]{1,0:T(8,128)(2,1)S(1)} %bitcast.11), custom_call_target="tpu_custom_call" | custom-call | flops 1073741824 | bytes 4325376 | tf_op jit(solution)/shard_map/near/pallas_call | solution.py:319
  35.5 0.7 %collective-permute-start.2 = (f32[512,256]{1,0:T(8,128)S(1)}, f32[512,256]{1,0:T(8,128)S(1)}, u32[]{:S(2)}, u32[]{:S(2)}) collective-permute-start(f32[512,256]{1,0:T(8,128)S(1)} %near.1), channel_id=1, source_target_pairs={{0,1},{1,0},{2,3},{3,2},{4,5},{5,4},{6,7},{7,6},{8,9},{9,8},{10,11... | collective-permute-start | bytes 1572872 | tf_op jit(solution)/shard_map/ppermute | solution.py:355
  36.2 0.0 copy-done
  36.2 1.0 %half.1 = f32[512,256]{1,0:T(8,128)S(1)} custom-call(bf16[512,3328]{1,0:T(8,128)(2,1)S(1)} %copy-done, bf16[2048,256]{1,0:T(8,128)(2,1)S(1)} %bitcast.8, bf16[384,256]{1,0:T(8,128)(2,1)S(1)} %bitcast.10, bf16[384,256]{1,0:T(8,128)(2,1)S(1)} %bitcast.12), custom_call_target="tpu_custom_call" | custom-call | flops 1073741824 | bytes 4849664 | tf_op jit(solution)/shard_map/half/pallas_call | solution.py:319
  37.2 0.6 %collective-permute-done.2 = f32[512,256]{1,0:T(8,128)S(1)} collective-permute-done((f32[512,256]{1,0:T(8,128)S(1)}, f32[512,256]{1,0:T(8,128)S(1)}, u32[]{:S(2)}, u32[]{:S(2)}) %collective-permute-start.2) | collective-permute-done | bytes 524320 | tf_op jit(solution)/shard_map/ppermute | solution.py:355
  37.8 0.1 multiply_convert_fusion
  37.8 15.7 %all_to_all.10 = bf16[8,64,256]{2,1,0:T(8,128)(2,1)S(1)} all-to-all(bf16[8,64,256]{2,1,0:T(8,128)(2,1)S(1)} %bitcast.14), channel_id=1, replica_groups={{0,2,4,6,8,10,12,14},{1,3,5,7,9,11,13,15},{16,18,20,22,24,26,28,30},{17..., dimensions={0} | all-to-all | bytes 524288 | tf_op jit(solution)/shard_map/all_to_all | solution.py:361
  53.6 0.7 %convert_reduce_fusion = f32[64,256]{1,0:T(8,128)} fusion(bf16[8,64,256]{2,1,0:T(8,128)(2,1)S(1)} %all_to_all.10), kind=kLoop, calls=%fused_computation | loop fusion | flops 245760 | bytes 327680 | tf_op jit(solution)/shard_map/reduce_sum | solution.py:362
Async XLA Ops:
  0.0 11.2 %copy-start.3 = (s32[24]{0:T(128)S(1)}, s32[24]{0:T(128)}, u32[]{:S(2)}) copy-start(s32[24]{0:T(128)} %exponents.1) | copy-start | bytes 292
  0.0 11.2 %copy-start.4 = (s32[4,24]{1,0:T(4,128)S(1)}, s32[4,24]{1,0:T(4,128)}, u32[]{:S(2)}) copy-start(s32[4,24]{1,0:T(4,128)} %counts_in.1) | copy-start | bytes 1156
  0.0 11.2 %copy-start.2 = (s32[4,24,6]{1,0,2:T(4,128)S(1)}, s32[4,24,6]{1,0,2:T(4,128)}, u32[]{:S(2)}) copy-start(s32[4,24,6]{1,0,2:T(4,128)} %param.10) | copy-start | bytes 6916
  2.7 30.3 %all-to-all-start = ((bf16[16,128,256]{2,1,0:T(8,128)(2,1)}), bf16[16,128,256]{2,1,0:T(8,128)(2,1)S(1)}, u32[]{:S(2)}, u32[]{:S(2)}) async-start(bf16[16,128,256]{2,1,0:T(8,128)(2,1)} %get-tuple-element.12), calls=%async_computation | async-start | bytes 2097152 | tf_op jit(solution)/shard_map/all_to_all | solution.py:342
  10.1 23.3 %collective-permute-start = (bf16[3,128,256]{2,1,0:T(8,128)(2,1)}, bf16[3,128,256]{2,1,0:T(8,128)(2,1)S(1)}, u32[]{:S(2)}, u32[]{:S(2)}) collective-permute-start(bf16[3,128,256]{2,1,0:T(8,128)(2,1)} %get-tuple-element.14), channel_id=1, source_target_pairs={{0,1},{1,0},{2,3},{3,2},{4,5},{5,4},{6,7},{7,6},{8,9},{9,8},{10,11... | collective-permute-start | bytes 589832 | tf_op jit(solution)/shard_map/ppermute | solution.py:344
  10.5 22.9 %collective-permute-start.1 = (bf16[3,128,256]{2,1,0:T(8,128)(2,1)}, bf16[3,128,256]{2,1,0:T(8,128)(2,1)S(1)}, u32[]{:S(2)}, u32[]{:S(2)}) collective-permute-start(bf16[3,128,256]{2,1,0:T(8,128)(2,1)} %get-tuple-element.15), channel_id=1, source_target_pairs={{1,2},{2,1},{3,4},{4,3},{5,6},{6,5},{7,8},{8,7},{9,10},{10,9},{11,... | collective-permute-start | bytes 589832 | tf_op jit(solution)/shard_map/ppermute | solution.py:343
  33.0 1.7 %copy-start.1 = (bf16[512,2560]{1,0:T(8,128)(2,1)S(1)}, bf16[512,2560]{1,0:T(8,128)(2,1)}, u32[]{:S(2)}) copy-start(bf16[512,2560]{1,0:T(8,128)(2,1)} %get-tuple-element.13.weights) | copy-start | bytes 7864324
  33.4 2.8 %copy-start = (bf16[512,3328]{1,0:T(8,128)(2,1)S(1)}, bf16[512,3328]{1,0:T(8,128)(2,1)}, u32[]{:S(2)}) copy-start(bf16[512,3328]{1,0:T(8,128)(2,1)} %get-tuple-element.16.weights) | copy-start | bytes 10223620
  35.5 2.2 %collective-permute-start.2 = (f32[512,256]{1,0:T(8,128)S(1)}, f32[512,256]{1,0:T(8,128)S(1)}, u32[]{:S(2)}, u32[]{:S(2)}) collective-permute-start(f32[512,256]{1,0:T(8,128)S(1)} %near.1), channel_id=1, source_target_pairs={{0,1},{1,0},{2,3},{3,2},{4,5},{5,4},{6,7},{7,6},{8,9},{9,8},{10,11... | collective-permute-start | bytes 1572872 | tf_op jit(solution)/shard_map/ppermute | solution.py:355
